TPU v7x, 512 devices: a whole 4x4x16 slice. The times are simulated.
512 devices in a mesh: expert: 32 (over y, z_lo, core), dp: 16 (over z_hi, x).
Axes of the slice: x: 4, y: 4, z: 16 (z_hi: 4, z_lo: 4; z = z_hi * 4 + z_lo), core: 2. Of those that a mesh axis runs over, the one named last changes fastest.
Arguments:
- hidden_acts: bfloat16 [4096, 4, 1024], P('expert', None, 'dp'), may hold values from -6 to 6
- expert_ids: int32 [4096, 4], P('expert'), may hold values from 0 to 31, all different within a row; in each aligned block of 128 rows (0 to 127, 128 to 255, ...) at most 32 rows name the same one
- gate_weights: float32 [4096, 4], P('expert'), may hold values from 0.05 to 0.6
- cotangent: bfloat16 [4096, 3584], P('expert', 'dp'), may hold values from -6 to 6
- weight_old: bfloat16 [32, 4864, 1024], P('expert', 'dp'), may hold values from -0.1875 to 0.1875
- first_old: bfloat16 [32, 4864, 1024], P('expert', 'dp'), may hold values from -30 to 30
- second_old: bfloat16 [32, 4864, 1024], P('expert', 'dp'), may hold values from 20 to 400
- old_place: int32 [3584], replicated, may hold values from 0 to 3647, as said below
- new_place: int32 [3584], replicated, may hold values from 0 to 3583, as said below
Outputs:
- combined: bfloat16 [4096, 3584], P('expert', 'dp')
- weight_new: bfloat16 [32, 3584, 1024], P('expert', 'dp')
- first_new: bfloat16 [32, 3584, 1024], P('expert', 'dp')
- second_new: bfloat16 [32, 3584, 1024], P('expert', 'dp')
Inputs may be any that keep to these rules, and one draw needn't show every extreme that they name: `expert_ids`: within the rows of one device each expert is named by at most 32 slots, a bound that some block reaches; the slots of one token name distinct experts. `new_place`: each new slot once. New slot q lies on dp device q // 224. `old_place`: distinct old slots. Old slot p lies on dp device p // 304, which is below 12. Of the rows that one old device holds, at most 19 go to any one new device, and exactly 19 for some pair of devices.
All inputs are finite; a program needn't handle non-finite values.
Results may differ from a plain program's by a relative error of at most 0.0049.
Values may be sent and summed in bfloat16 or wider, within the bound.
No kernel may reach another device: no remote copies, remote signals or barrier semaphores. Data moves between devices by JAX's collectives and lax.ppermute only.
A program may use at most 64 MiB of HBM per device.

v0:
```python
import jax
import jax.numpy as jnp
from jax import lax
from jax.sharding import PartitionSpec as P

beta_one = 0.9
beta_two = 0.95
adam_eps = 1e-08
learn_rate = 0.001
weight_decay = 0.1
bias_one = 1.0 - 0.9**50 * 0.9**50
bias_two = 1.0 - 0.95**50 * 0.95**50


def adamw_step(weight, moment_one, second, gradient):
    weight_wide = weight.astype(jnp.float32)
    one_next = beta_one * moment_one.astype(jnp.float32) + (1.0 - beta_one) * gradient
    two_next = beta_two * second.astype(jnp.float32) + (1.0 - beta_two) * gradient * gradient
    update = (
        one_next / bias_one / (jnp.sqrt(two_next / bias_two) + adam_eps)
        + weight_decay * weight_wide
    )
    return (
        (weight_wide - learn_rate * update).astype(jnp.bfloat16),
        one_next.astype(jnp.bfloat16),
        two_next.astype(jnp.bfloat16),
    )


def running_rank(labels, classes):
    onehot = (jnp.arange(classes, dtype=jnp.int32)[:, None] == labels[None, :]).astype(jnp.int32)
    return jnp.sum((jnp.cumsum(onehot, axis=1) - onehot) * onehot, axis=0)


def shards(
    hidden_acts,
    expert_ids,
    gate_weights,
    cotangent,
    weight_old,
    first_old,
    second_old,
    old_place,
    new_place,
):
    n_expert = lax.axis_size("expert")
    n_data = lax.axis_size("dp")
    data_index = lax.axis_index("dp")
    tok_rows, top_count, piece_width = hidden_acts.shape
    hidden = weight_old.shape[2]
    slice_width = cotangent.shape[1]
    model_width = slice_width * n_data
    old_group = 3 * n_data // 4
    move_cap = (slice_width + old_group - 1) // old_group
    old_rows = weight_old.shape[1]
    capacity = 2 * tok_rows * top_count // n_expert
    slot_count = tok_rows * top_count
    src_dev = old_place // old_rows
    src_pos = old_place % old_rows
    dst_dev = new_place // slice_width
    dst_pos = new_place % slice_width
    mine_out = src_dev == data_index
    mine_in = dst_dev == data_index
    send_rank = running_rank(jnp.where(mine_out, dst_dev, -1), n_data)
    recv_rank = running_rank(jnp.where(mine_in, src_dev, -1), old_group)
    send_slot = jnp.where(mine_out, dst_dev * move_cap + send_rank, n_data * move_cap)
    send_from = (
        jnp.full((n_data * move_cap,), old_rows, jnp.int32).at[send_slot].set(src_pos, mode="drop")
    )
    recv_slot = jnp.where(mine_in, dst_pos, slice_width)
    recv_from = (
        jnp.zeros((slice_width,), jnp.int32)
        .at[recv_slot]
        .set(src_dev * move_cap + recv_rank, mode="drop")
    )

    def pack_state(source):
        padded = jnp.concatenate([source[0], jnp.zeros((1, hidden), source.dtype)], axis=0)
        return jnp.take(padded, send_from, axis=0).reshape(n_data, move_cap, hidden)

    def unpack_state(received):
        return jnp.take(received.reshape(n_data * move_cap, hidden), recv_from, axis=0)

    regrouped = (
        lax.all_to_all(pack_state(weight_old), "dp", split_axis=0, concat_axis=0, tiled=True),
        lax.all_to_all(pack_state(first_old), "dp", split_axis=0, concat_axis=0, tiled=True),
        lax.all_to_all(pack_state(second_old), "dp", split_axis=0, concat_axis=0, tiled=True),
    )
    weight_now = unpack_state(regrouped[0])
    first_now = unpack_state(regrouped[1])
    second_now = unpack_state(regrouped[2])
    flat_ids = expert_ids.reshape(slot_count)
    slot_of = flat_ids * capacity + running_rank(flat_ids, n_expert)
    source_of = (
        jnp.full((n_expert * capacity,), slot_count, jnp.int32)
        .at[slot_of]
        .set(jnp.arange(slot_count, dtype=jnp.int32))
    )
    inverse = (
        jnp.zeros((model_width,), jnp.int32)
        .at[new_place]
        .set(jnp.arange(model_width, dtype=jnp.int32))
    )
    inverse_block = lax.dynamic_slice_in_dim(inverse, data_index * slice_width, slice_width)
    place_block = lax.dynamic_slice_in_dim(new_place, data_index * slice_width, slice_width)

    def slot_rows(values):
        padded = jnp.concatenate([values, jnp.zeros((1, values.shape[1]), values.dtype)], axis=0)
        return jnp.take(padded, source_of, axis=0).reshape(n_expert, capacity, values.shape[1])

    whole_acts, full_cot = (
        lax.all_gather(hidden_acts, "dp", axis=2, tiled=True),
        lax.all_gather(cotangent, "dp", axis=1, tiled=True),
    )
    chosen = jnp.take(full_cot, inverse_block, axis=1)
    scaled = (gate_weights[:, :, None] * chosen[:, None, :].astype(jnp.float32)).astype(
        jnp.bfloat16
    )
    arrived_acts = lax.all_to_all(
        slot_rows(whole_acts.reshape(slot_count, hidden)),
        "expert",
        split_axis=0,
        concat_axis=0,
        tiled=True,
    )
    arrived_scaled = lax.all_to_all(
        slot_rows(scaled.reshape(slot_count, slice_width)),
        "expert",
        split_axis=0,
        concat_axis=0,
        tiled=True,
    )
    rows_all = arrived_acts.reshape(-1, hidden)
    scaled_rows = arrived_scaled.reshape(-1, slice_width)
    outputs = lax.dot_general(
        rows_all, weight_now, (((1,), (1,)), ((), ())), preferred_element_type=jnp.float32
    ).astype(jnp.bfloat16)
    returned = lax.all_to_all(
        outputs.reshape(n_expert, capacity, slice_width),
        "expert",
        split_axis=0,
        concat_axis=0,
        tiled=True,
    )
    per_slot = jnp.take(
        returned.reshape(n_expert * capacity, slice_width), slot_of, axis=0
    ).reshape(tok_rows, top_count, slice_width)
    combined_part = jnp.sum(gate_weights[:, :, None] * per_slot.astype(jnp.float32), axis=1).astype(
        jnp.bfloat16
    )
    new_order = lax.all_gather(combined_part, "dp", axis=1, tiled=True)
    combined = jnp.take(new_order, place_block, axis=1)
    gradient = lax.dot_general(
        scaled_rows, rows_all, (((0,), (0,)), ((), ())), preferred_element_type=jnp.float32
    )
    new_weight, new_one, new_two = adamw_step(weight_now, first_now, second_now, gradient)
    return (combined, new_weight[None], new_one[None], new_two[None])


def solution(mesh):
    return jax.shard_map(
        shards,
        mesh=mesh,
        in_specs=(
            P("expert", None, "dp"),
            P("expert", None),
            P("expert", None),
            P("expert", "dp"),
            P("expert", "dp", None),
            P("expert", "dp", None),
            P("expert", "dp", None),
            P(),
            P(),
        ),
        out_specs=(
            P("expert", "dp"),
            P("expert", "dp", None),
            P("expert", "dp", None),
            P("expert", "dp", None),
        ),
        check_vma=False,
    )
```

profile of v0, /device:TPU:24, one launch (start us, length us, event | category | flops | bytes accessed | tf_op | source)
XLA Modules:
  0.0 503.4 jit_solution(17578476946292517152)
XLA Ops:
  7.2 0.7 broadcast_multiply_fusion
  7.9 0.8 copy.34
  9.0 1.2 reduce-window.20
  10.6 2.4 scatter_custom_fusion
  13.1 0.8 copy.33
  13.9 74.1 %all_gather.11 = bf16[128,3584]{0,1:T(8,128)(2,1)S(1)} all-gather(bf16[128,224]{0,1:T(8,128)(2,1)} %param.18), channel_id=1, replica_groups=mesh['expert'=32,'dp'=16] {'dp'}, dimensions={1}, use_global_device_ids=true | all-gather | bytes 974848 | tf_op jit(solution)/shard_map/all_gather | solution.py:113
  88.0 0.8 compare_select_fusion
  88.8 13.7 %scatter_custom_fusion.3 = s32[3584]{0:T(1024)S(1)} fusion(s32[3584]{0:T(1024)S(1)} %get-tuple-element.16, s32[3584]{0:T(1024)S(1)} %iota.40, s32[]{:T(128)} %constant.95.clone.1), kind=kCustom, calls=%fused_computation.77 | custom fusion | bytes 14340 | tf_op jit(solution)/shard_map/scatter | solution.py:102
  102.6 0.8 gather_fusion.8
  104.2 3.9 gather_fusion.2
  108.1 1.0 broadcast_select_fusion.4
  109.1 4.9 all-to-all-start.4
  114.2 4.6 reduce-window.24
  119.8 13.6 %scatter_custom_fusion.1 = s32[304]{0:T(512)S(1)} fusion(s32[3584]{0:T(1024)S(1)} %get-tuple-element.15, s32[3584]{0:T(1024)S(1)} %get-tuple-element.18, s32[]{:T(128)} %constant.108.clone.1), kind=kCustom, calls=%fused_computation.98 | custom fusion | bytes 1220 | tf_op jit(solution)/shard_map/scatter | solution.py:68
  133.4 2.1 gather_fusion.9
  135.5 2.1 gather_fusion.6
  137.7 2.1 gather_fusion.3
  139.8 1.1 broadcast_select_fusion.1
  140.9 1.1 reshape.205
  141.9 13.9 %all-to-all-start.1 = ((bf16[16,19,1024]{2,1,0:T(8,128)(2,1)}), bf16[16,19,1024]{2,1,0:T(8,128)(2,1)S(1)}, u32[]{:S(2)}, u32[]{:S(2)}) async-start(bf16[16,19,1024]{2,1,0:T(8,128)(2,1)} %reshape.205), calls=%async_computation.1 | async-start | bytes 1572864 | tf_op jit(solution)/shard_map/all_to_all | solution.py:85
  155.9 1.1 reshape.212
  157.0 23.6 %all-to-all-done.1 = bf16[16,19,1024]{2,1,0:T(8,128)(2,1)S(1)} async-done(((bf16[16,19,1024]{2,1,0:T(8,128)(2,1)}), bf16[16,19,1024]{2,1,0:T(8,128)(2,1)S(1)}, u32[]{:S(2)}, u32[]{:S(2)}) %all-to-all-start.1) | async-done | bytes 622624 | tf_op jit(solution)/shard_map/all_to_all | solution.py:85
  180.6 25.4 %all-to-all-start.5 = ((bf16[16,19,1024]{2,1,0:T(8,128)(2,1)}), bf16[16,19,1024]{2,1,0:T(8,128)(2,1)}, u32[]{:S(2)}, u32[]{:S(2)}) async-start(bf16[16,19,1024]{2,1,0:T(8,128)(2,1)} %reshape.212), calls=%async_computation.5 | async-start | bytes 1572864 | tf_op jit(solution)/shard_map/all_to_all | solution.py:87
  206.0 0.7 all-gather.2.cloned.1.call-update
  206.7 88.9 %all-gather.2.cloned.1.call-done = bf16[128,4,1024]{0,2,1:T(8,128)(2,1)} async-done(((bf16[128,4,64]{0,2,1:T(8,128)(2,1)}), bf16[128,4,1024]{0,2,1:T(8,128)(2,1)}) %all-gather.2.cloned.1.call-update) | async-done | bytes 1048592 | tf_op jit(solution)/shard_map/all_gather | solution.py:112
  295.7 1.9 copy.38
  297.9 4.1 gather_fusion
  302.0 1.6 broadcast_select_fusion
  303.5 5.2 %all-to-all-start = ((bf16[32,32,1024]{2,1,0:T(8,128)(2,1)}), bf16[32,32,1024]{2,1,0:T(8,128)(2,1)}, u32[]{:S(2)}, u32[]{:S(2)}) async-start(bf16[32,32,1024]{2,1,0:T(8,128)(2,1)} %broadcast_select_fusion), calls=%async_computation | async-start | bytes 4194304 | tf_op jit(solution)/shard_map/all_to_all | solution.py:119
  308.8 1.1 reshape.210
  309.9 47.1 %all-to-all-done = bf16[32,32,1024]{2,1,0:T(8,128)(2,1)} async-done(((bf16[32,32,1024]{2,1,0:T(8,128)(2,1)}), bf16[32,32,1024]{2,1,0:T(8,128)(2,1)}, u32[]{:S(2)}, u32[]{:S(2)}) %all-to-all-start) | async-done | bytes 2097184 | tf_op jit(solution)/shard_map/all_to_all | solution.py:119
  357.0 8.9 %all-to-all-start.3 = ((bf16[16,19,1024]{2,1,0:T(8,128)(2,1)}), bf16[16,19,1024]{2,1,0:T(8,128)(2,1)S(1)}, u32[]{:S(2)}, u32[]{:S(2)}) async-start(bf16[16,19,1024]{2,1,0:T(8,128)(2,1)} %reshape.210), calls=%async_computation.3 | async-start | bytes 1572864 | tf_op jit(solution)/shard_map/all_to_all | solution.py:86
  365.9 3.5 reduce-window.26
  370.1 13.6 %scatter_custom_fusion.2 = s32[224]{0:T(256)S(1)} fusion(s32[3584]{0:T(1024)S(1)} %get-tuple-element.19, s32[3584]{0:T(1024)S(1)} %bitcast_add_fusion.1, s32[]{:T(128)} %constant.95.clone.1), kind=kCustom, calls=%fused_computation.101 | custom fusion | bytes 900 | tf_op jit(solution)/shard_map/scatter | solution.py:74
  384.0 1.1 gather_fusion.4
  385.1 2.4 convolution_convert_fusion
  387.6 1.0 copy.39
  388.6 16.6 %all-to-all-done.3 = bf16[16,19,1024]{2,1,0:T(8,128)(2,1)S(1)} async-done(((bf16[16,19,1024]{2,1,0:T(8,128)(2,1)}), bf16[16,19,1024]{2,1,0:T(8,128)(2,1)S(1)}, u32[]{:S(2)}, u32[]{:S(2)}) %all-to-all-start.3) | async-done | bytes 622624 | tf_op jit(solution)/shard_map/all_to_all | solution.py:86
  405.2 8.9 %all-to-all-start.2 = ((bf16[32,32,224]{2,1,0:T(8,128)(2,1)}), bf16[32,32,224]{2,1,0:T(8,128)(2,1)S(1)}, u32[]{:S(2)}, u32[]{:S(2)}) async-start(bf16[32,32,224]{2,1,0:T(8,128)(2,1)} %bitcast.9), calls=%async_computation.2 | async-start | bytes 1048576 | tf_op jit(solution)/shard_map/all_to_all | solution.py:138
  414.5 1.4 reshape.213
  415.8 1.1 gather_fusion.10
  417.2 1.1 gather_fusion.7
  418.3 4.3 fusion.6
  422.5 6.0 %all-to-all-done.2 = bf16[32,32,224]{2,1,0:T(8,128)(2,1)S(1)} async-done(((bf16[32,32,224]{2,1,0:T(8,128)(2,1)}), bf16[32,32,224]{2,1,0:T(8,128)(2,1)S(1)}, u32[]{:S(2)}, u32[]{:S(2)}) %all-to-all-start.2) | async-done | bytes 458784 | tf_op jit(solution)/shard_map/all_to_all | solution.py:138
  428.5 1.9 gather_fusion.1
  431.2 63.9 %all_gather.10 = bf16[128,3584]{0,1:T(8,128)(2,1)S(1)} all-gather(bf16[128,224]{0,1:T(8,128)(2,1)S(1)} %copy.40), channel_id=1, replica_groups=mesh['expert'=32,'dp'=16] {'dp'}, dimensions={1}, use_global_device_ids=true | all-gather | bytes 974848 | tf_op jit(solution)/shard_map/all_gather | solution.py:151
  495.1 0.8 gather_fusion.5
  495.9 0.7 select_bitcast_fusion
  (77 shorter events, 5.4 us)
Async XLA Ops:
  108.1 6.0 %copy-start.3 = (bf16[1,304,1024]{2,1,0:T(8,128)(2,1)S(1)}, bf16[1,304,1024]{2,1,0:T(8,128)(2,1)}, u32[]{:S(2)}) copy-start(bf16[1,304,1024]{2,1,0:T(8,128)(2,1)} %param.21) | copy-start | bytes 1867780
  108.1 11.4 %copy-start.4 = (bf16[1,304,1024]{2,1,0:T(8,128)(2,1)S(1)}, bf16[1,304,1024]{2,1,0:T(8,128)(2,1)}, u32[]{:S(2)}) copy-start(bf16[1,304,1024]{2,1,0:T(8,128)(2,1)} %param.20) | copy-start | bytes 1867780
  109.1 32.8 %all-to-all-start.4 = ((bf16[32,32,224]{2,1,0:T(8,128)(2,1)}), bf16[32,32,224]{2,1,0:T(8,128)(2,1)}, u32[]{:S(2)}, u32[]{:S(2)}) async-start(bf16[32,32,224]{2,1,0:T(8,128)(2,1)} %broadcast_select_fusion.4), calls=%async_computation.4 | async-start | bytes 1048576 | tf_op jit(solution)/shard_map/all_to_all | solution.py:126
  114.1 5.6 %copy-start.6 = (s32[3584]{0:T(1024)S(1)}, s32[3584]{0:T(1024)}, u32[]{:S(2)}) copy-start(s32[3584]{0:T(1024)} %param.22) | copy-start | bytes 43012
  114.1 5.6 %copy-start.7 = (s32[3584]{0:T(1024)S(1)}, s32[3584]{0:T(1024)}, u32[]{:S(2)}) copy-start(s32[3584]{0:T(1024)} %param.23) | copy-start | bytes 43012
  135.5 2.1 copy-start.5
  141.9 38.7 %all-to-all-start.1 = ((bf16[16,19,1024]{2,1,0:T(8,128)(2,1)}), bf16[16,19,1024]{2,1,0:T(8,128)(2,1)S(1)}, u32[]{:S(2)}, u32[]{:S(2)}) async-start(bf16[16,19,1024]{2,1,0:T(8,128)(2,1)} %reshape.205), calls=%async_computation.1 | async-start | bytes 1572864 | tf_op jit(solution)/shard_map/all_to_all | solution.py:85
  180.6 115.0 %copy-start = (bf16[16,19,1024]{2,1,0:T(8,128)(2,1)}, bf16[16,19,1024]{2,1,0:T(8,128)(2,1)S(1)}, u32[]{:S(2)}) copy-start(bf16[16,19,1024]{2,1,0:T(8,128)(2,1)S(1)} %all-to-all-done.1) | copy-start | bytes 1867780
  180.6 122.9 %all-to-all-start.5 = ((bf16[16,19,1024]{2,1,0:T(8,128)(2,1)}), bf16[16,19,1024]{2,1,0:T(8,128)(2,1)}, u32[]{:S(2)}, u32[]{:S(2)}) async-start(bf16[16,19,1024]{2,1,0:T(8,128)(2,1)} %reshape.212), calls=%async_computation.5 | async-start | bytes 1572864 | tf_op jit(solution)/shard_map/all_to_all | solution.py:87
  206.0 89.7 %all-gather.2.cloned.1.call-start = ((), (), s32[]{:S(2)}) async-start(), calls=%async_computation.6 | async-start | bytes 1114112 | tf_op jit(solution)/shard_map/all_gather | solution.py:112
  303.5 5.2 %copy-start.2 = (bf16[304,1024]{1,0:T(8,128)(2,1)S(1)}, bf16[304,1024]{1,0:T(8,128)(2,1)}, u32[]{:S(2)}) copy-start(bf16[304,1024]{1,0:T(8,128)(2,1)} %get-tuple-element.21) | copy-start | bytes 1867780
  303.5 53.5 %all-to-all-start = ((bf16[32,32,1024]{2,1,0:T(8,128)(2,1)}), bf16[32,32,1024]{2,1,0:T(8,128)(2,1)}, u32[]{:S(2)}, u32[]{:S(2)}) async-start(bf16[32,32,1024]{2,1,0:T(8,128)(2,1)} %broadcast_select_fusion), calls=%async_computation | async-start | bytes 4194304 | tf_op jit(solution)/shard_map/all_to_all | solution.py:119
  308.8 75.0 %copy-start.1 = (bf16[16,19,1024]{2,1,0:T(8,128)(2,1)S(1)}, bf16[16,19,1024]{2,1,0:T(8,128)(2,1)}, u32[]{:S(2)}) copy-start(bf16[16,19,1024]{2,1,0:T(8,128)(2,1)} %copy-done) | copy-start | bytes 1867780
  357.0 48.2 %all-to-all-start.3 = ((bf16[16,19,1024]{2,1,0:T(8,128)(2,1)}), bf16[16,19,1024]{2,1,0:T(8,128)(2,1)S(1)}, u32[]{:S(2)}, u32[]{:S(2)}) async-start(bf16[16,19,1024]{2,1,0:T(8,128)(2,1)} %reshape.210), calls=%async_computation.3 | async-start | bytes 1572864 | tf_op jit(solution)/shard_map/all_to_all | solution.py:86
  385.1 29.1 %copy-start.8 = (s32[128,4]{0,1:T(4,128)S(1)}, s32[128,4]{0,1:T(4,128)}, u32[]{:S(2)}) copy-start(s32[128,4]{0,1:T(4,128)} %param.16) | copy-start | bytes 6148
  405.2 23.3 %all-to-all-start.2 = ((bf16[32,32,224]{2,1,0:T(8,128)(2,1)}), bf16[32,32,224]{2,1,0:T(8,128)(2,1)S(1)}, u32[]{:S(2)}, u32[]{:S(2)}) async-start(bf16[32,32,224]{2,1,0:T(8,128)(2,1)} %bitcast.9), calls=%async_computation.2 | async-start | bytes 1048576 | tf_op jit(solution)/shard_map/all_to_all | solution.py:138
Sparse Core Ops, SparseCore 0:
  209.8 85.7 all-gather.1
where the time goes:
time: 508 us; the launch traced here: 503 us
  waiting for transfers between devices  183 us (36%)
  blocking collectives  138 us (27%)
  local copies, waits for them, and re-layouts  77.1 us (15%)
  starting transfers between devices  67.2 us (13%)
  other arithmetic  17 us (3%)
  between operations  14.6 us (3%)
  matrix products  6.71 us (1%)
    all_gather x1, waiting for transfers between devices, shards(): lax.all_gather(hidden_acts, 'dp', axis=2, tiled=True)  88.9 us
    all_gather x1, blocking collectives, shards(): lax.all_gather(cotangent, 'dp', axis=1, tiled=True)  74.1 us
    all_gather x1, blocking collectives, shards(): new_order = lax.all_gather(combined_part, 'dp', axis=1, tiled=True)  63.9 us
    all_to_all x1, waiting for transfers between devices, shards(): lax.all_to_all(slot_rows(whole_acts.reshape(slot_count, hidden)), 'expert...  47.1 us
    all_to_all x1, starting transfers between devices, shards(): lax.all_to_all(pack_state(second_old), 'dp', split_axis=0, concat_axis=0,...  25.4 us
    all_to_all x1, waiting for transfers between devices, shards(): lax.all_to_all(pack_state(weight_old), 'dp', split_axis=0, concat_axis=0,...  23.6 us
    all_to_all x1, waiting for transfers between devices, shards(): lax.all_to_all(pack_state(first_old), 'dp', split_axis=0, concat_axis=0,...  16.6 us
    all_to_all x1, starting transfers between devices, shards(): lax.all_to_all(pack_state(weight_old), 'dp', split_axis=0, concat_axis=0,...  13.9 us
  transfers between devices with their start and end apart: 7, of which 5 were waited for; matrix products, arithmetic and copies ran while one was open for 14% of the time, Pallas kernels for 0%

commit v1 on v0

v1 whole, which is shorter than its diff:
```python
import jax
import jax.numpy as jnp
from jax import lax
from jax.experimental import pallas as pl
from jax.experimental.pallas import tpu as pltpu
from jax.sharding import PartitionSpec as P

beta_one = 0.9
beta_two = 0.95
adam_eps = 1e-08
learn_rate = 0.001
weight_decay = 0.1
bias_one = 1.0 - 0.9**50 * 0.9**50
bias_two = 1.0 - 0.95**50 * 0.95**50

RING = 4
NEAR = [[far * RING + near for near in range(RING)] for far in range(RING)]
FAR = [[far * RING + near for far in range(RING)] for near in range(RING)]

VMEM_BYTES = 48 * 1024 * 1024
CONTRACT_LAST = (((1,), (1,)), ((), ()))
CONTRACT_FIRST = (((0,), (0,)), ((), ()))


def dot(left, right, dims=(((1,), (0,)), ((), ()))):
    return lax.dot_general(left, right, dims, preferred_element_type=jnp.float32)


def whole():
    return pl.BlockSpec(memory_space=pltpu.VMEM)


def gather_dp(piece):
    far = lax.all_gather(piece, "dp", axis=0, axis_index_groups=FAR)
    return lax.all_gather(far, "dp", axis=0, axis_index_groups=NEAR)


def forward_kernel(acts_ref, weight_ref, rows_ref, out_ref):
    near, far, rows, lanes = acts_ref.shape
    half = lanes // 2
    source = lax.broadcasted_iota(jnp.int32, (2 * lanes, lanes), 0)
    target = lax.broadcasted_iota(jnp.int32, (2 * lanes, lanes), 1)
    picked = jnp.where(target < half, target, target + half)
    shuffles = [(source == picked + side * half).astype(jnp.bfloat16) for side in range(2)]
    for z in range(far):
        for x in range(0, near, 2):
            pair = jnp.concatenate([acts_ref[x, z], acts_ref[x + 1, z]], axis=1)
            first = (z * near + x) * half
            for side in range(2):
                rows_ref[side, :, first : first + lanes] = dot(pair, shuffles[side]).astype(
                    jnp.bfloat16
                )
    for side in range(2):
        result = dot(rows_ref[side], weight_ref[...], CONTRACT_LAST).astype(jnp.bfloat16)
        blocks, slots, width = out_ref.shape
        out_ref[:, side * (slots // 2) : (side + 1) * (slots // 2), :] = result.reshape(
            blocks, slots // 2, width
        )


def update_kernel(rows_ref, scaled_ref, weight_ref, moments_ref, place_ref, w_ref, m_ref, v_ref):
    blocks, slots, width = scaled_ref.shape
    half = slots // 2
    unpack = place_ref[...]
    lanes = 256
    for first in range(0, w_ref.shape[1], lanes):
        piece = slice(first, first + lanes)
        gradient = jnp.zeros((width, lanes), jnp.float32)
        for side in range(2):
            scaled = scaled_ref[:, side * half : (side + 1) * half, :].reshape(blocks * half, width)
            gradient += dot(scaled, rows_ref[side, :, piece], CONTRACT_FIRST)
        weight = weight_ref[:, piece].astype(jnp.float32)
        one = dot(unpack, moments_ref[0, :, piece])
        two = dot(unpack, moments_ref[1, :, piece])
        one_next = beta_one * one + (1.0 - beta_one) * gradient
        two_next = beta_two * two + (1.0 - beta_two) * gradient * gradient
        update = (
            one_next / bias_one / (jnp.sqrt(two_next / bias_two) + adam_eps)
            + weight_decay * weight
        )
        w_ref[:, piece] = (weight - learn_rate * update).astype(jnp.bfloat16)
        m_ref[:, piece] = one_next.astype(jnp.bfloat16)
        v_ref[:, piece] = two_next.astype(jnp.bfloat16)


def shards(
    hidden_acts,
    expert_ids,
    gate_weights,
    cotangent,
    weight_old,
    first_old,
    second_old,
    old_place,
    new_place,
):
    n_expert = lax.axis_size("expert")
    n_data = lax.axis_size("dp")
    me = lax.axis_index("dp")
    tok_rows, top_count, piece_width = hidden_acts.shape
    hidden = weight_old.shape[2]
    width = cotangent.shape[1]
    model_width = width * n_data
    old_group = 3 * n_data // 4
    move_cap = (width + old_group - 1) // old_group
    old_rows = weight_old.shape[1]
    slot_count = tok_rows * top_count
    cap = 2 * slot_count // n_expert
    bf16 = jnp.bfloat16

    def count(size):
        return jnp.arange(size, dtype=jnp.int32)

    ids = expert_ids.reshape(slot_count)
    earlier = (ids[:, None] == ids[None, :]) & (count(slot_count)[None, :] < count(slot_count)[:, None])
    slot_of = ids * cap + jnp.sum(earlier.astype(jnp.int32), axis=1)
    row = count(n_expert * cap // 2)
    low = row // (cap // 2) * cap + row % (cap // 2)
    acts_flat = hidden_acts.reshape(slot_count, piece_width)
    sides = [
        dot((low[:, None] + side * (cap // 2) == slot_of[None, :]).astype(bf16), acts_flat).astype(bf16)
        for side in range(2)
    ]
    packed = jnp.concatenate(sides, axis=1).reshape(n_expert, cap // 2, 2 * piece_width)
    arrived = lax.all_to_all(packed, "expert", split_axis=0, concat_axis=0, tiled=True)

    moved = old_place[None, :] == me * old_rows + count(old_rows)[:, None]
    new_of_old = jnp.sum(jnp.where(moved, new_place[None, :] + 1, 0), axis=1) - 1
    target = jnp.where(new_of_old >= 0, new_of_old // width, n_data)
    before = (target[:, None] == target[None, :]) & (count(old_rows)[None, :] < count(old_rows)[:, None])
    send_slot = jnp.where(
        target < n_data, target * move_cap + jnp.sum(before.astype(jnp.int32), axis=1), -1
    )
    pack = (count(n_data * move_cap)[:, None] == send_slot[None, :]).astype(bf16)

    held = new_place[None, :] == me * width + count(width)[:, None]
    model_row = jnp.sum(jnp.where(held, count(model_width)[None, :], 0), axis=1)
    origin = jnp.sum(jnp.where(held, old_place[None, :], 0), axis=1)
    owner = origin // old_rows
    lower = (owner[:, None] == owner[None, :]) & (origin[None, :] < origin[:, None])
    recv_slot = owner * move_cap + jnp.sum(lower.astype(jnp.int32), axis=1)
    unpack = (recv_slot[:, None] == count(n_data * move_cap)[None, :]).astype(bf16)

    def pack_state(source):
        return dot(pack, source[0]).astype(bf16).reshape(n_data, move_cap, hidden)

    weight_got = lax.all_to_all(
        pack_state(weight_old), "dp", split_axis=0, concat_axis=0, tiled=True
    ).reshape(n_data * move_cap, hidden)
    moments = jnp.concatenate([pack_state(first_old), pack_state(second_old)], axis=1)
    moments_got = lax.all_to_all(moments, "dp", split_axis=0, concat_axis=0, tiled=True)
    moments_got = (
        moments_got.reshape(n_data, 2, move_cap, hidden)
        .transpose(1, 0, 2, 3)
        .reshape(2, n_data * move_cap, hidden)
    )

    ring = n_data // RING
    block = (count(ring)[None, :] * RING + count(RING)[:, None]).reshape(n_data)
    column = block[:, None] * width + count(width)[None, :]

    def pick(blocks, wanted):
        hot = (column[:, :, None] == wanted[None, None, :]).astype(bf16)
        return jnp.einsum(
            "jtc,jcn->tn",
            blocks.reshape(n_data, tok_rows, width),
            hot,
            preferred_element_type=jnp.float32,
        )

    chosen = pick(gather_dp(cotangent), model_row).astype(bf16)
    gates = gate_weights.reshape(slot_count)
    places = count(n_expert * cap)[:, None] == slot_of[None, :]
    gate_packed = jnp.sum(jnp.where(places, gates[None, :], 0.0), axis=1)
    token_of = jnp.max(
        jnp.where(
            count(n_expert * cap)[:, None, None] == slot_of.reshape(tok_rows, top_count).T[None], 1, 0
        ),
        axis=1,
    ).astype(bf16)
    scaled = (gate_packed[:, None] * dot(token_of, chosen)).astype(bf16)
    scaled_got = lax.all_to_all(
        scaled.reshape(n_expert, cap, width), "expert", split_axis=0, concat_axis=0, tiled=True
    )

    weight_now = dot(unpack, weight_got).astype(bf16)
    acts_all = gather_dp(arrived.reshape(n_expert * cap // 2, 2 * piece_width))
    rows, outputs = pl.pallas_call(
        forward_kernel,
        out_shape=(
            jax.ShapeDtypeStruct((2, n_expert * cap // 2, hidden), bf16),
            jax.ShapeDtypeStruct((n_expert, cap, width), bf16),
        ),
        in_specs=[whole()] * 2,
        out_specs=(whole(), whole()),
        compiler_params=pltpu.CompilerParams(vmem_limit_bytes=VMEM_BYTES),
        cost_estimate=pl.CostEstimate(
            flops=2 * n_expert * cap * hidden * (width + 512),
            bytes_accessed=5 * 1024 * 1024,
            transcendentals=0,
        ),
        name="forward",
    )(acts_all, weight_now)
    returned = lax.all_to_all(outputs, "expert", split_axis=0, concat_axis=0, tiled=True)
    mine = (slot_of[:, None] == count(n_expert * cap)[None, :]).astype(bf16)
    per_slot = dot(mine, returned.reshape(n_expert * cap, width)).reshape(tok_rows, top_count, width)
    combined_part = jnp.sum(gate_weights[:, :, None] * per_slot, axis=1).astype(bf16)
    place_block = lax.dynamic_slice_in_dim(new_place, me * width, width)
    combined = pick(gather_dp(combined_part), place_block).astype(bf16)

    state = jax.ShapeDtypeStruct((width, hidden), bf16)
    new_weight, new_one, new_two = pl.pallas_call(
        update_kernel,
        out_shape=(state, state, state),
        in_specs=[whole()] * 5,
        out_specs=(whole(), whole(), whole()),
        compiler_params=pltpu.CompilerParams(vmem_limit_bytes=VMEM_BYTES),
        cost_estimate=pl.CostEstimate(
            flops=2 * n_expert * cap * hidden * width,
            bytes_accessed=6 * 1024 * 1024,
            transcendentals=width * hidden,
        ),
        name="update",
    )(rows, scaled_got, weight_now, moments_got, unpack)
    return (combined, new_weight[None], new_one[None], new_two[None])


def solution(mesh):
    return jax.shard_map(
        shards,
        mesh=mesh,
        in_specs=(
            P("expert", None, "dp"),
            P("expert", None),
            P("expert", None),
            P("expert", "dp"),
            P("expert", "dp", None),
            P("expert", "dp", None),
            P("expert", "dp", None),
            P(),
            P(),
        ),
        out_specs=(
            P("expert", "dp"),
            P("expert", "dp", None),
            P("expert", "dp", None),
            P("expert", "dp", None),
        ),
        check_vma=False,
    )
```

time: 508 us -> 355 us (0.70)
  waiting for transfers between devices: 183 us -> 89 us
  local copies, waits for them, and re-layouts: 77.1 us -> 14.2 us
  blocking collectives: 138 us -> 171 us
  starting transfers between devices: 67.2 us -> 46.5 us
  other arithmetic: 17 us -> 4.61 us
    all_gather x1, waiting for transfers between devices: 88.9 us -> 33.8 us  [gather_dp(): return lax.all_gather(far, 'dp', axis=0, axis_index_groups=NEAR)]
    all_to_all x5 -> x4, waiting for transfers between devices: 69.7 us -> 19.8 us  [the longest x1 11.9 us: shards(): lax.all_to_all(scaled.reshape(n_expert, cap, width), 'expert', split_axis...]
    scatter x4 -> x0, local copies, waits for them, and re-layouts: 43.4 us -> none  [the longest x1 13.7 us: shards(): inverse = jnp.zeros((model_width,), jnp.int32).at[new_place].set(jnp.aran...]
    all_gather x2 -> x5, blocking collectives: 138 us -> 171 us  [the longest x3 142 us: gather_dp(): far = lax.all_gather(piece, 'dp', axis=0, axis_index_groups=FAR)]
    gather x12 -> x0, local copies, waits for them, and re-layouts: 21.2 us -> none  [the longest x2 8.01 us: slot_rows(): jnp.take(padded, source_of, axis=0)]
    all_to_all x5 -> x4, starting transfers between devices: 53.2 us -> 36.9 us  [the longest x1 10.9 us: shards(): lax.all_to_all(scaled.reshape(n_expert, cap, width), 'expert', split_axis...]
    all_to_all x1, waiting for transfers between devices: 23.6 us -> 35.4 us  [shards(): lax.all_to_all(pack_state(weight_old), 'dp', split_axis=0, concat_axis=0,...]
    another operation x6 -> x0, other arithmetic: 9.66 us -> none
  transfers between devices with their start and end apart: 7 -> 6, of which waited for: 5 -> 4; matrix products, arithmetic and copies ran while one was open for 14% -> 5% of each run, Pallas kernels for 0% -> 1%
where the time goes in v1:
time: 355 us
  blocking collectives  171 us (48%)
  waiting for transfers between devices  89 us (25%)
  starting transfers between devices  46.5 us (13%)
  between operations  14.4 us (4%)
  local copies, waits for them, and re-layouts  14.2 us (4%)
  matrix products  10 us (3%)
  Pallas kernels  4.65 us (1%)
  other arithmetic  4.61 us (1%)
    all_gather x3, blocking collectives, gather_dp(): far = lax.all_gather(piece, 'dp', axis=0, axis_index_groups=FAR)  142 us
    all_to_all x1, waiting for transfers between devices, shards(): lax.all_to_all(pack_state(weight_old), 'dp', split_axis=0, concat_axis=0,...  35.4 us
    all_gather x1, waiting for transfers between devices, gather_dp(): return lax.all_gather(far, 'dp', axis=0, axis_index_groups=NEAR)  33.8 us
    all_gather x2, blocking collectives, gather_dp(): return lax.all_gather(far, 'dp', axis=0, axis_index_groups=NEAR)  28.9 us
    all_to_all x1, waiting for transfers between devices, shards(): lax.all_to_all(scaled.reshape(n_expert, cap, width), 'expert', split_axis...  11.9 us
    all_to_all x1, starting transfers between devices, shards(): lax.all_to_all(scaled.reshape(n_expert, cap, width), 'expert', split_axis...  10.9 us
    all_to_all x1, starting transfers between devices, shards(): lax.all_to_all(pack_state(weight_old), 'dp', split_axis=0, concat_axis=0,...  9.52 us
    all_to_all x1, starting transfers between devices, shards(): lax.all_to_all(packed, 'expert', split_axis=0, concat_axis=0, tiled=True)  9.26 us
  transfers between devices with their start and end apart: 6, of which 4 were waited for; matrix products, arithmetic and copies ran while one was open for 5% of the time, Pallas kernels for 1%

profile of v1, /device:TPU:24, one launch (start us, length us, event | category | flops | bytes accessed | tf_op | source)
XLA Modules:
  0.0 354.6 jit_solution(3471952270775053796)
XLA Ops:
  7.3 1.0 copy.76
  8.3 0.8 copy.74
  9.2 0.3 convert_reduce_fusion
  9.5 0.4 convolution_convert_fusion.4
  9.9 0.4 convolution_convert_fusion.5
  10.3 0.8 copy.77
  11.1 9.3 %all-to-all-start = ((bf16[32,16,128]{2,1,0:T(8,128)(2,1)}), bf16[32,16,128]{2,1,0:T(8,128)(2,1)S(1)}, u32[]{:S(2)}, u32[]{:S(2)}) async-start(bf16[32,16,128]{2,1,0:T(8,128)(2,1)} %bitcast.2), calls=%async_computation | async-start | bytes 262144 | tf_op jit(solution)/shard_map/all_to_all | solution.py:125
  20.6 28.6 %all-gather.3 = bf16[512,224]{0,1:T(8,128)(2,1)S(1)} all-gather(bf16[128,224]{0,1:T(8,128)(2,1)S(1)} %copy-done.10), channel_id=5, replica_groups={{0,4,8,12},{1,5,9,13},{2,6,10,14},{3,7,11,15},{16,20,24,28},{17,21,25,2..., dimensions={0}, use_global_device_ids=true | all-gather | bytes 286720 | tf_op jit(solution)/shard_map/all_gather | solution.py:34
  49.2 14.1 %all-gather.4 = bf16[16,128,224]{1,2,0:T(8,128)(2,1)S(1)} all-gather(bf16[4,128,224]{1,2,0:T(8,128)(2,1)S(1)} %copy_bitcast_fusion), channel_id=6, replica_groups={{0,1,2,3},{4,5,6,7},{8,9,10,11},{12,13,14,15},{16,17,18,19},{20,21,22,2..., dimensions={0}, use_global_device_ids=true | all-gather | bytes 1146880 | tf_op jit(solution)/shard_map/all_gather | solution.py:35
  63.3 0.1 copy.80
  63.5 0.3 select_reduce_fusion.2
  63.8 1.0 fusion.5
  64.9 0.3 select_reduce_fusion.1
  65.3 1.3 fusion.13
  66.6 1.0 copy.82
  67.6 10.9 %all-to-all-start.3 = ((bf16[32,32,224]{2,1,0:T(8,128)(2,1)}), bf16[32,32,224]{2,1,0:T(8,128)(2,1)S(1)}, u32[]{:S(2)}, u32[]{:S(2)}) async-start(bf16[32,32,224]{2,1,0:T(8,128)(2,1)} %bitcast.11), calls=%async_computation.3 | async-start | bytes 1048576 | tf_op jit(solution)/shard_map/all_to_all | solution.py:182
  78.6 0.6 select_reduce_fusion
  79.2 0.2 convert_reduce_fusion.1
  79.5 0.5 convolution_convert_fusion.2
  80.0 1.1 reshape.249
  81.1 11.9 %all-to-all-done.3.scaled_ref = bf16[32,32,224]{2,1,0:T(8,128)(2,1)S(1)} async-done(((bf16[32,32,224]{2,1,0:T(8,128)(2,1)}), bf16[32,32,224]{2,1,0:T(8,128)(2,1)S(1)}, u32[]{:S(2)}, u32[]{:S(2)}) %all-to-all-start.3) | async-done | bytes 458784 | tf_op jit(solution)/shard_map/all_to_all | solution.py:182
  93.0 9.5 %all-to-all-start.1 = ((bf16[16,19,1024]{2,1,0:T(8,128)(2,1)}), bf16[16,19,1024]{2,1,0:T(8,128)(2,1)S(1)}, u32[]{:S(2)}, u32[]{:S(2)}) async-start(bf16[16,19,1024]{2,1,0:T(8,128)(2,1)} %reshape.249), calls=%async_computation.1 | async-start | bytes 1572864 | tf_op jit(solution)/shard_map/all_to_all | solution.py:147
  102.6 0.5 convolution_convert_fusion
  103.1 0.2 reshape.256
  103.3 2.4 convolution_convert_fusion.1
  105.7 1.3 reshape.255
  107.0 1.4 pad_maximum_fusion
  108.3 35.4 %all-to-all-done.1 = bf16[16,19,1024]{2,1,0:T(8,128)(2,1)S(1)} async-done(((bf16[16,19,1024]{2,1,0:T(8,128)(2,1)}), bf16[16,19,1024]{2,1,0:T(8,128)(2,1)S(1)}, u32[]{:S(2)}, u32[]{:S(2)}) %all-to-all-start.1) | async-done | bytes 622624 | tf_op jit(solution)/shard_map/all_to_all | solution.py:147
  143.7 8.7 %all-to-all-start.4 = ((bf16[16,38,1024]{2,1,0:T(8,128)(2,1)}), bf16[16,38,1024]{2,1,0:T(8,128)(2,1)}, u32[]{:S(2)}, u32[]{:S(2)}) async-start(bf16[16,38,1024]{2,1,0:T(8,128)(2,1)} %pad_maximum_fusion), calls=%async_computation.4 | async-start | bytes 2621440 | tf_op jit(solution)/shard_map/all_to_all | solution.py:151
  152.5 84.2 %all_gather.31 = bf16[4,512,128]{2,1,0:T(8,128)(2,1)} all-gather(bf16[1,512,128]{2,1,0:T(8,128)(2,1)S(1)} %bitcast.61), channel_id=1, replica_groups={{0,4,8,12},{1,5,9,13},{2,6,10,14},{3,7,11,15},{16,20,24,28},{17,21,25,2..., dimensions={0}, use_global_device_ids=true | all-gather | bytes 655360 | tf_op jit(solution)/shard_map/all_gather | solution.py:34
  236.7 0.2 convert_reduce_fusion.2
  237.0 0.2 reshape.250
  237.2 1.2 convolution_convert_fusion.3.weight_ref
  238.4 33.8 %all-gather.7.cloned.1.call-done = bf16[16,512,128]{2,1,0:T(8,128)(2,1)} async-done(((bf16[4,512,128]{2,1,0:T(8,128)(2,1)}), bf16[16,512,128]{2,1,0:T(8,128)(2,1)}) %all-gather.7.cloned.1.call-update) | async-done | bytes 2097168 | tf_op jit(solution)/shard_map/all_gather | solution.py:35
  272.2 1.0 copy-done.1
  273.3 1.6 copy-done.4
  274.8 1.8 forward.1
  276.7 0.8 copy-done.3
  277.4 8.0 %all-to-all-start.2 = ((bf16[32,32,224]{2,1,0:T(8,128)(2,1)}), bf16[32,32,224]{2,1,0:T(8,128)(2,1)}, u32[]{:S(2)}, u32[]{:S(2)}) async-start(bf16[32,32,224]{2,1,0:T(8,128)(2,1)} %copy-done.3), calls=%async_computation.2 | async-start | bytes 1048576 | tf_op jit(solution)/shard_map/all_to_all | solution.py:204
  285.7 2.0 copy.83
  287.7 1.3 copy.84
  289.0 0.3 copy.85.moments_ref
  289.3 2.9 update.1
  292.2 7.8 %all-to-all-done.2 = bf16[32,32,224]{2,1,0:T(8,128)(2,1)} async-done(((bf16[32,32,224]{2,1,0:T(8,128)(2,1)}), bf16[32,32,224]{2,1,0:T(8,128)(2,1)}, u32[]{:S(2)}, u32[]{:S(2)}) %all-to-all-start.2) | async-done | bytes 458784 | tf_op jit(solution)/shard_map/all_to_all | solution.py:204
  300.0 1.7 fusion.17
  301.7 29.6 %all-gather.1 = bf16[512,224]{0,1:T(8,128)(2,1)S(1)} all-gather(bf16[128,224]{0,1:T(8,128)(2,1)S(1)} %fusion.17), channel_id=3, replica_groups={{0,4,8,12},{1,5,9,13},{2,6,10,14},{3,7,11,15},{16,20,24,28},{17,21,25,2..., dimensions={0}, use_global_device_ids=true | all-gather | bytes 286720 | tf_op jit(solution)/shard_map/all_gather | solution.py:34
  331.3 14.8 %all-gather.2 = bf16[16,128,224]{1,2,0:T(8,128)(2,1)S(1)} all-gather(bf16[4,128,224]{1,2,0:T(8,128)(2,1)S(1)} %copy_bitcast_fusion.1), channel_id=4, replica_groups={{0,1,2,3},{4,5,6,7},{8,9,10,11},{12,13,14,15},{16,17,18,19},{20,21,22,2..., dimensions={0}, use_global_device_ids=true | all-gather | bytes 1146880 | tf_op jit(solution)/shard_map/all_gather | solution.py:35
  346.2 1.6 fusion.29
  (51 shorter events, 1.1 us)
Async XLA Ops:
  7.2 72.3 %copy-start = (bf16[1,304,1024]{2,1,0:T(8,128)(2,1)S(1)}, bf16[1,304,1024]{2,1,0:T(8,128)(2,1)}, u32[]{:S(2)}) copy-start(bf16[1,304,1024]{2,1,0:T(8,128)(2,1)} %param.13) | copy-start | bytes 1867780
  7.2 13.4 %copy-start.11 = (s32[128,4]{0,1:T(4,128)S(1)}, s32[128,4]{0,1:T(4,128)}, u32[]{:S(2)}) copy-start(s32[128,4]{0,1:T(4,128)} %param.10) | copy-start | bytes 6148
  7.2 13.4 %copy-start.10 = (bf16[128,224]{0,1:T(8,128)(2,1)S(1)}, bf16[128,224]{0,1:T(8,128)(2,1)}, u32[]{:S(2)}) copy-start(bf16[128,224]{0,1:T(8,128)(2,1)} %param.12) | copy-start | bytes 172036
  7.2 56.1 %copy-start.12 = (f32[128,4]{0,1:T(4,128)S(1)}, f32[128,4]{0,1:T(4,128)}, u32[]{:S(2)}) copy-start(f32[128,4]{0,1:T(4,128)} %param.11) | copy-start | bytes 6148
  7.2 56.6 %copy-start.8 = (s32[3584]{0:T(1024)S(1)}, s32[3584]{0:T(1024)}, u32[]{:S(2)}) copy-start(s32[3584]{0:T(1024)} %param.17) | copy-start | bytes 43012
  7.2 56.6 %copy-start.9 = (s32[3584]{0:T(1024)S(1)}, s32[3584]{0:T(1024)}, u32[]{:S(2)}) copy-start(s32[3584]{0:T(1024)} %param.16) | copy-start | bytes 43012
  11.1 56.6 %all-to-all-start = ((bf16[32,16,128]{2,1,0:T(8,128)(2,1)}), bf16[32,16,128]{2,1,0:T(8,128)(2,1)S(1)}, u32[]{:S(2)}, u32[]{:S(2)}) async-start(bf16[32,16,128]{2,1,0:T(8,128)(2,1)} %bitcast.2), calls=%async_computation | async-start | bytes 262144 | tf_op jit(solution)/shard_map/all_to_all | solution.py:125
  67.6 11.8 %copy-start.6 = (bf16[32,16,128]{2,1,0:T(8,128)(2,1)}, bf16[32,16,128]{2,1,0:T(8,128)(2,1)S(1)}, u32[]{:S(2)}) copy-start(bf16[32,16,128]{2,1,0:T(8,128)(2,1)S(1)} %all-to-all-done) | copy-start | bytes 393220
  67.6 25.4 %all-to-all-start.3 = ((bf16[32,32,224]{2,1,0:T(8,128)(2,1)}), bf16[32,32,224]{2,1,0:T(8,128)(2,1)S(1)}, u32[]{:S(2)}, u32[]{:S(2)}) async-start(bf16[32,32,224]{2,1,0:T(8,128)(2,1)} %bitcast.11), calls=%async_computation.3 | async-start | bytes 1048576 | tf_op jit(solution)/shard_map/all_to_all | solution.py:182
  79.5 23.1 %copy-start.5 = (bf16[1,304,1024]{2,1,0:T(8,128)(2,1)S(1)}, bf16[1,304,1024]{2,1,0:T(8,128)(2,1)}, u32[]{:S(2)}) copy-start(bf16[1,304,1024]{2,1,0:T(8,128)(2,1)} %param.15) | copy-start | bytes 1867780
  93.0 50.7 %all-to-all-start.1 = ((bf16[16,19,1024]{2,1,0:T(8,128)(2,1)}), bf16[16,19,1024]{2,1,0:T(8,128)(2,1)S(1)}, u32[]{:S(2)}, u32[]{:S(2)}) async-start(bf16[16,19,1024]{2,1,0:T(8,128)(2,1)} %reshape.249), calls=%async_computation.1 | async-start | bytes 1572864 | tf_op jit(solution)/shard_map/all_to_all | solution.py:147
  108.3 44.2 %copy-start.7 = (bf16[32,16,128]{2,1,0:T(8,128)(2,1)S(1)}, bf16[32,16,128]{2,1,0:T(8,128)(2,1)}, u32[]{:S(2)}) copy-start(bf16[32,16,128]{2,1,0:T(8,128)(2,1)} %copy-done.6) | copy-start | bytes 393220
  143.7 133.7 %all-to-all-start.4 = ((bf16[16,38,1024]{2,1,0:T(8,128)(2,1)}), bf16[16,38,1024]{2,1,0:T(8,128)(2,1)}, u32[]{:S(2)}, u32[]{:S(2)}) async-start(bf16[16,38,1024]{2,1,0:T(8,128)(2,1)} %pad_maximum_fusion), calls=%async_computation.4 | async-start | bytes 2621440 | tf_op jit(solution)/shard_map/all_to_all | solution.py:151
  152.4 119.8 %all-gather.7.cloned.1.call-start = ((), (), s32[]{:S(2)}) async-start(), calls=%async_computation.5 | async-start | bytes 2621440 | tf_op jit(solution)/shard_map/all_gather | solution.py:35
  272.2 1.0 copy-start.1
  273.3 1.6 copy-start.4
  276.7 0.8 copy-start.3
  277.4 22.5 %all-to-all-start.2 = ((bf16[32,32,224]{2,1,0:T(8,128)(2,1)}), bf16[32,32,224]{2,1,0:T(8,128)(2,1)}, u32[]{:S(2)}, u32[]{:S(2)}) async-start(bf16[32,32,224]{2,1,0:T(8,128)(2,1)} %copy-done.3), calls=%async_computation.2 | async-start | bytes 1048576 | tf_op jit(solution)/shard_map/all_to_all | solution.py:204
  287.7 1.6 copy-start.2
Sparse Core Ops, SparseCore 0:
  236.8 35.3 all-gather.6

commit v2 on v1

v2 whole, which is shorter than its diff:
```python
import jax
import jax.numpy as jnp
from jax import lax
from jax.experimental import pallas as pl
from jax.experimental.pallas import tpu as pltpu
from jax.sharding import PartitionSpec as P

beta_one = 0.9
beta_two = 0.95
adam_eps = 1e-08
learn_rate = 0.001
weight_decay = 0.1
bias_one = 1.0 - 0.9**50 * 0.9**50
bias_two = 1.0 - 0.95**50 * 0.95**50

RING = 4
NEAR = [[far * RING + near for near in range(RING)] for far in range(RING)]
FAR = [[far * RING + near for far in range(RING)] for near in range(RING)]

LANES = 128
CHUNKS = 8
ROWS = 16

VMEM_BYTES = 48 * 1024 * 1024
CONTRACT_LAST = (((1,), (1,)), ((), ()))
CONTRACT_FIRST = (((0,), (0,)), ((), ()))


def dot(left, right, dims=(((1,), (0,)), ((), ()))):
    return lax.dot_general(left, right, dims, preferred_element_type=jnp.float32)


def whole():
    return pl.BlockSpec(memory_space=pltpu.VMEM)


def gather_far(piece):
    return lax.all_gather(piece, "dp", axis=0, axis_index_groups=FAR)


def gather_near(piece):
    return lax.all_gather(piece, "dp", axis=0, axis_index_groups=NEAR)


def gather_whole(piece):
    every = lax.all_gather(piece, "dp", axis=0)
    return every.reshape(RING, RING, *piece.shape).swapaxes(0, 1)


def send_far(piece, step):
    pairs = [
        (far * RING + near, (far + step) % RING * RING + near)
        for far in range(RING)
        for near in range(RING)
    ]
    return lax.ppermute(piece, "dp", pairs)


def iota(shape, axis):
    return lax.broadcasted_iota(jnp.int32, shape, axis)


def to_row(column):
    size = column.shape[0]
    same = iota((size, size), 0) == iota((size, size), 1)
    return jnp.sum(jnp.where(same, column, 0), axis=0, keepdims=True)


def pick(blocks_ref, wanted):
    near, far, width, tokens = blocks_ref.shape
    column = iota((wanted.shape[0], width), 1)
    total = jnp.zeros((wanted.shape[0], tokens), jnp.float32)
    for x in range(near):
        for z in range(far):
            hot = (column + (z * near + x) * width == wanted).astype(jnp.bfloat16)
            total += dot(hot, blocks_ref[x, z])
    return total


def slot_hot(slot_ref, slots):
    top, tokens = slot_ref.shape
    here = iota((slots, tokens), 0)
    return jnp.concatenate(
        [(here == slot_ref[k : k + 1, :]).astype(jnp.bfloat16) for k in range(top)], axis=1
    )


def dispatch_kernel(acts_ref, ids_ref, packed_ref, slot_ref):
    experts, half, wide = packed_ref.shape
    top, tokens = ids_ref.shape
    piece, cap = wide // 2, 2 * half
    every = top * tokens
    choices = jnp.concatenate([ids_ref[k : k + 1, :] for k in range(top)], axis=1)
    named = iota((experts, every), 0) == choices
    ahead = (iota((every, every), 0) < iota((every, every), 1)).astype(jnp.bfloat16)
    rank = dot(named.astype(jnp.bfloat16), ahead)
    rank = jnp.sum(jnp.where(named, rank, 0.0), axis=0, keepdims=True).astype(jnp.int32)
    slot = choices * cap + rank
    for k in range(top):
        slot_ref[k : k + 1, :] = slot[:, k * tokens : (k + 1) * tokens]
    features = jnp.concatenate(
        [acts_ref[k * piece : (k + 1) * piece, :] for k in range(top)], axis=1
    )
    row = iota((experts * half, every), 0)
    row = row // half * cap + row % half
    sides = [
        dot((row + side * half == slot).astype(jnp.bfloat16), features, CONTRACT_LAST)
        for side in range(2)
    ]
    packed = jnp.concatenate(sides, axis=1).astype(jnp.bfloat16)
    packed_ref[...] = packed.reshape(packed_ref.shape)


def scale_kernel(blocks_ref, wanted_ref, gates_ref, slot_ref, packed_ref):
    experts, cap, width = packed_ref.shape
    top = gates_ref.shape[0]
    chosen = pick(blocks_ref, wanted_ref[...])
    scaled = jnp.concatenate(
        [(gates_ref[k : k + 1, :] * chosen).astype(jnp.bfloat16) for k in range(top)], axis=1
    )
    hot = slot_hot(slot_ref, experts * cap)
    packed_ref[...] = dot(hot, scaled, CONTRACT_LAST).astype(jnp.bfloat16).reshape(packed_ref.shape)


def tables(me, old_ref, new_ref, old_rows, width, cap):
    blocks, lanes = old_ref.shape
    far = me // RING
    leaving = jnp.zeros((old_rows, lanes), jnp.int32)
    origin = jnp.zeros((width, lanes), jnp.int32)
    model = jnp.zeros((width, lanes), jnp.int32)
    own = jnp.zeros((width, lanes), jnp.int32)
    for i in range(blocks):
        old, new = old_ref[i : i + 1, :], new_ref[i : i + 1, :]
        number = iota((1, lanes), 1) + i * lanes
        leaving += jnp.where(old - me * old_rows == iota((old_rows, lanes), 0), new + 1, 0)
        row = iota((width, lanes), 0)
        held = new - me * width == row
        origin += jnp.where(held, old, 0)
        model += jnp.where(held, number, 0)
        own += jnp.where(number - me * width == row, new, 0)
    leaving, origin, model, own = [
        jnp.sum(part, axis=1, keepdims=True) for part in (leaving, origin, model, own)
    ]
    leaving_row = to_row(leaving)
    target, target_row = (leaving - 1) // width, (leaving_row - 1) // width
    size = (old_rows, old_rows)
    rank = jnp.sum(
        ((target == target_row) & (iota(size, 0) < iota(size, 1)) & (leaving > 0)).astype(jnp.int32),
        axis=0,
        keepdims=True,
    )
    step = (target_row // RING - far + RING) % RING
    first = target_row % RING * RING
    send = jnp.where(leaving_row > 0, (first + target_row // RING) * cap + rank, -1)
    send_step = jnp.where(leaving_row > 0, (first + step) * cap + rank, -1)
    origin_row = to_row(origin)
    owner, owner_row = origin // old_rows, origin_row // old_rows
    rank = jnp.sum(
        ((owner == owner_row) & (origin_row < origin)).astype(jnp.int32), axis=1, keepdims=True
    )
    step = (far - owner // RING + RING) % RING
    recv = owner * cap + rank
    recv_step = (step * RING + owner % RING) * cap + rank
    return send, send_step, recv, recv_step, model, own


def pack_lines(source, slot, devices, cap):
    count = source.shape[0]
    rest = cap - ROWS
    lines = rest * CHUNKS
    index = iota((devices * ROWS, count), 0)
    hot = (index // ROWS * cap + index % ROWS == slot).astype(jnp.bfloat16)
    main = dot(hot, source)
    index = iota((devices * lines, count), 0)
    hot = (index // lines * cap + ROWS + index % rest == slot).astype(jnp.bfloat16)
    tail_rows = dot(hot, source)
    line = iota((devices * lines, LANES), 0) % lines // rest
    tail = jnp.zeros((devices * lines, LANES), jnp.float32)
    for c in range(CHUNKS):
        tail = jnp.where(line == c, tail_rows[:, c * LANES : (c + 1) * LANES], tail)
    mains = [main[:, c * LANES : (c + 1) * LANES].reshape(devices, ROWS, LANES) for c in range(CHUNKS)]
    return mains, tail.reshape(devices, lines, LANES)


def pack_kernel(me_ref, old_ref, new_ref, *refs):
    sources, (out_ref, recv_ref, recv_step_ref, model_ref, own_ref, held, sems) = refs[:3], refs[3:]
    copies = [pltpu.make_async_copy(source, held.at[i], sems.at[i]) for i, source in enumerate(sources)]
    for copy in copies:
        copy.start()
    devices, lines, _ = out_ref.shape
    cap = lines // (CHUNKS * len(sources))
    send, send_step, recv_ref[...], recv_step_ref[...], model_ref[...], own_ref[...] = tables(
        me_ref[0], old_ref, new_ref, held.shape[1], recv_ref.shape[0], cap
    )
    for copy in copies:
        copy.wait()
    place, tails = 0, []
    for number in range(len(sources)):
        mains, tail = pack_lines(held[number], send_step if number else send, devices, cap)
        for main in mains:
            out_ref[:, place : place + ROWS, :] = main.astype(jnp.bfloat16)
            place += ROWS
        tails.append(tail)
    out_ref[:, place:, :] = jnp.concatenate(tails, axis=1).astype(jnp.bfloat16)


class Arrived:
    def __init__(self, refs, recv, count):
        devices = sum(ref.shape[0] for ref in refs)
        lines = refs[0].shape[1]
        cap = lines // (CHUNKS * count)
        self.refs = refs
        width = recv.shape[0]
        rest = cap - ROWS
        self.lines = rest * CHUNKS
        index = iota((width, devices * ROWS), 1)
        self.main = (index // ROWS * cap + index % ROWS == recv).astype(jnp.bfloat16)
        index = iota((width, devices * self.lines), 1)
        self.tail = (index // self.lines * cap + ROWS + index % rest == recv).astype(jnp.bfloat16)
        self.chunk = iota((devices * self.lines, LANES), 0) % self.lines // rest
        start = count * CHUNKS * ROWS
        self.rest = jnp.concatenate([ref[:, start:, :].astype(jnp.float32) for ref in refs], axis=0)

    def piece(self, number, c):
        first = (number * CHUNKS + c) * ROWS
        rows = [ref[:, first : first + ROWS, :].reshape(-1, LANES) for ref in self.refs]
        rest = self.rest[:, number * self.lines : (number + 1) * self.lines, :].reshape(-1, LANES)
        rest = jnp.where(self.chunk == c, rest, 0.0).astype(jnp.bfloat16)
        return dot(self.main, jnp.concatenate(rows, axis=0)) + dot(self.tail, rest)


def unpack_kernel(got_ref, recv_ref, weight_ref):
    arrived = Arrived([got_ref], recv_ref[...], 1)
    for c in range(CHUNKS):
        weight_ref[:, c * LANES : (c + 1) * LANES] = arrived.piece(0, c).astype(jnp.bfloat16)


def forward_kernel(acts_ref, weight_ref, rows_ref, out_ref):
    near, far, rows, lanes = acts_ref.shape
    half = lanes // 2
    source, target = iota((2 * lanes, lanes), 0), iota((2 * lanes, lanes), 1)
    picked = jnp.where(target < half, target, target + half)
    shuffles = [(source == picked + side * half).astype(jnp.bfloat16) for side in range(2)]
    for z in range(far):
        for x in range(0, near, 2):
            pair = jnp.concatenate([acts_ref[x, z], acts_ref[x + 1, z]], axis=1)
            first = (z * near + x) * half
            for side in range(2):
                rows_ref[side, :, first : first + lanes] = dot(pair, shuffles[side]).astype(
                    jnp.bfloat16
                )
    blocks, slots, width = out_ref.shape
    for side in range(2):
        result = dot(rows_ref[side], weight_ref[...], CONTRACT_LAST).astype(jnp.bfloat16)
        out_ref[:, side * (slots // 2) : (side + 1) * (slots // 2), :] = result.reshape(
            blocks, slots // 2, width
        )


def combine_kernel(returned_ref, gates_ref, slot_ref, out_ref):
    experts, cap, width = returned_ref.shape
    top, tokens = gates_ref.shape
    rows = returned_ref[...].reshape(experts * cap, width)
    each = dot(rows, slot_hot(slot_ref, experts * cap), CONTRACT_FIRST)
    total = jnp.zeros((width, tokens), jnp.float32)
    for k in range(top):
        total += gates_ref[k : k + 1, :] * each[:, k * tokens : (k + 1) * tokens]
    out_ref[...] = total.astype(jnp.bfloat16)


def pick_kernel(blocks_ref, wanted_ref, out_ref):
    out_ref[...] = pick(blocks_ref, wanted_ref[...]).astype(jnp.bfloat16)


def gradient_kernel(rows_ref, scaled_ref, out_ref):
    blocks, slots, width = scaled_ref.shape
    half = slots // 2
    total = jnp.zeros(out_ref.shape, jnp.float32)
    for side in range(2):
        scaled = scaled_ref[:, side * half : (side + 1) * half, :].reshape(blocks * half, width)
        total += dot(scaled, rows_ref[side], CONTRACT_FIRST)
    out_ref[...] = total


def update_kernel(gradient_ref, weight_ref, *refs):
    recv_ref, w_ref, m_ref, v_ref = refs[RING:]
    arrived = Arrived(refs[:RING], recv_ref[...], 2)
    for c in range(CHUNKS):
        piece = slice(c * LANES, (c + 1) * LANES)
        gradient = gradient_ref[:, piece]
        weight = weight_ref[:, piece].astype(jnp.float32)
        one_next = beta_one * arrived.piece(0, c) + (1.0 - beta_one) * gradient
        two_next = beta_two * arrived.piece(1, c) + (1.0 - beta_two) * gradient * gradient
        update = (
            one_next / bias_one / (jnp.sqrt(two_next / bias_two) + adam_eps)
            + weight_decay * weight
        )
        w_ref[:, piece] = (weight - learn_rate * update).astype(jnp.bfloat16)
        m_ref[:, piece] = one_next.astype(jnp.bfloat16)
        v_ref[:, piece] = two_next.astype(jnp.bfloat16)


def call(kernel, name, out_shape, *args, flops=0, scalars=0, apart=(), scratch=(), order=()):
    several = isinstance(out_shape, tuple)
    count = len(args)

    def body(*refs):
        kernel(*refs[:count], *refs[count + len(order) :])

    specs = [pl.BlockSpec(memory_space=pltpu.SMEM)] * scalars + [whole()] * (count - scalars)
    for i in apart:
        specs[i] = pl.BlockSpec(memory_space=pltpu.HBM)
    return pl.pallas_call(
        body,
        out_shape=out_shape,
        in_specs=specs + [pl.BlockSpec(memory_space=pl.ANY)] * len(order),
        out_specs=tuple(whole() for _ in out_shape) if several else whole(),
        scratch_shapes=scratch,
        compiler_params=pltpu.CompilerParams(vmem_limit_bytes=VMEM_BYTES),
        cost_estimate=pl.CostEstimate(flops=flops, bytes_accessed=1024, transcendentals=0),
        name=name,
    )(*args, *order)


def shards(
    hidden_acts,
    expert_ids,
    gate_weights,
    cotangent,
    weight_old,
    first_old,
    second_old,
    old_place,
    new_place,
):
    n_expert = lax.axis_size("expert")
    n_data = lax.axis_size("dp")
    me = lax.axis_index("dp")
    tok_rows, top_count, piece = hidden_acts.shape
    hidden = weight_old.shape[2]
    width = cotangent.shape[1]
    old_group = 3 * n_data // 4
    move_cap = (width + old_group - 1) // old_group
    cap = 2 * tok_rows * top_count // n_expert
    slots = n_expert * cap
    int32 = jnp.int32

    def shape(*sizes, dtype=jnp.bfloat16):
        return jax.ShapeDtypeStruct(sizes, dtype)

    def exchange(array, axis, groups=None):
        return lax.all_to_all(
            array, axis, split_axis=0, concat_axis=0, tiled=True, axis_index_groups=groups
        )

    rows = slots // 2
    packed, slot = call(
        dispatch_kernel,
        "dispatch",
        (shape(n_expert, cap // 2, 2 * piece), shape(top_count, tok_rows, dtype=int32)),
        hidden_acts.transpose(1, 2, 0).reshape(top_count * piece, tok_rows),
        expert_ids.T,
    )
    arrived = exchange(packed, "expert")

    lines = hidden // LANES * move_cap
    old_rows = weight_old.shape[1]
    column = shape(width, 1, dtype=int32)
    sent, recv, recv_step, model, own = call(
        pack_kernel,
        "pack",
        (shape(n_data, 3 * lines, LANES), column, column, column, column),
        me[None].astype(int32),
        old_place.reshape(-1, LANES),
        new_place.reshape(-1, LANES),
        weight_old[0],
        first_old[0],
        second_old[0],
        scalars=1,
        apart=(3, 4, 5),
        scratch=[pltpu.VMEM((3, old_rows, hidden), jnp.bfloat16), pltpu.SemaphoreType.DMA((3,))],
    )
    sent, arrived = lax.optimization_barrier((sent, arrived))
    state = exchange(sent.reshape(RING, RING, 3 * lines, LANES), "dp", NEAR)

    both = jnp.concatenate([arrived.reshape(rows, 2 * piece), cotangent.T], axis=0)
    both_far, state = lax.optimization_barrier((gather_far(both), state))
    acts_all = gather_near(both_far[:, :rows])
    cot_far = both_far[:, rows:]
    gates = gate_weights.T

    block = ROWS * CHUNKS
    rest = lines - block
    weight_sent = jnp.concatenate(
        [state[:, :, :block], state[:, :, 3 * block : 3 * block + rest]], axis=2
    ).transpose(1, 0, 2, 3)
    weight_got = exchange(weight_sent, "dp", FAR).reshape(n_data, lines, LANES)
    weight_now = call(unpack_kernel, "unpack", shape(width, hidden), weight_got, recv)
    moments_got = []
    for step in range(RING):
        moments = jnp.concatenate(
            [state[:, step, block : 3 * block], state[:, step, 3 * block + rest :]], axis=1
        )
        moments_got.append(send_far(moments, step) if step else moments)

    def tail(gather):
        def run(acts_all, weight_now, cot_far, slot, gates, model, own):
            rows_now, outputs = call(
                forward_kernel,
                "forward",
                (shape(2, rows, hidden), shape(n_expert, cap, width)),
                acts_all,
                weight_now,
            )
            returned = exchange(outputs, "expert")
            scaled = call(
                scale_kernel,
                "scale",
                shape(n_expert, cap, width),
                gather_near(cot_far),
                model,
                gates,
                slot,
            )
            scaled, returned = lax.optimization_barrier((scaled, returned))
            scaled_got = exchange(scaled, "expert")
            part = call(combine_kernel, "combine", shape(width, tok_rows), returned, gates, slot)
            gradient = call(
                gradient_kernel,
                "gradient",
                shape(width, hidden, dtype=jnp.float32),
                rows_now,
                scaled_got,
            )
            combined = call(pick_kernel, "pick", shape(width, tok_rows), gather(part), own)
            return combined, gradient

        return run

    combined, gradient = lax.cond(
        new_place[0] >= 0,
        tail(lambda part: gather_near(gather_far(part))),
        tail(gather_whole),
        acts_all,
        weight_now,
        cot_far,
        slot,
        gates,
        model,
        own,
    )
    combined = combined.T
    new_weight, new_one, new_two = call(
        update_kernel,
        "update",
        (shape(width, hidden),) * 3,
        gradient,
        weight_now,
        *moments_got,
        recv_step,
    )
    return (combined, new_weight[None], new_one[None], new_two[None])


def solution(mesh):
    return jax.shard_map(
        shards,
        mesh=mesh,
        in_specs=(
            P("expert", None, "dp"),
            P("expert", None),
            P("expert", None),
            P("expert", "dp"),
            P("expert", "dp", None),
            P("expert", "dp", None),
            P("expert", "dp", None),
            P(),
            P(),
        ),
        out_specs=(
            P("expert", "dp"),
            P("expert", "dp", None),
            P("expert", "dp", None),
            P("expert", "dp", None),
        ),
        check_vma=False,
    )
```

time: 355 us -> 252 us (0.71)
  waiting for transfers between devices: 89 us -> 2.6 us
  blocking collectives: 171 us -> 95 us
  starting transfers between devices: 46.5 us -> 97.7 us
  Pallas kernels: 4.65 us -> 22.9 us
  matrix products: 10 us -> 0 us
    all_gather x5 -> x4, blocking collectives: 171 us -> 95 us  [the longest x2 60.6 us: gather_far(): return lax.all_gather(piece, 'dp', axis=0, axis_index_groups=FAR)]
    all_to_all x5, waiting for transfers between devices: 55.1 us -> 0.01 us  [exchange(): lax.all_to_all(array, axis, split_axis=0, concat_axis=0, tiled=True, axis...]
    all_gather x1, waiting for transfers between devices: 33.8 us -> 2.56 us  [gather_near(): return lax.all_gather(piece, 'dp', axis=0, axis_index_groups=NEAR)]
    all_to_all x5, starting transfers between devices: 46.4 us -> 75.2 us  [exchange(): lax.all_to_all(array, axis, split_axis=0, concat_axis=0, tiled=True, axis...]
    ppermute x0 -> x3, starting transfers between devices: none -> 22.5 us  [send_far(): return lax.ppermute(piece, 'dp', pairs)]
    pallas_call x2 -> x9, Pallas kernels: 4.65 us -> 22.9 us  [call(): pl.pallas_call(body, out_shape=out_shape, in_specs=specs + [pl.BlockSpec(...]
    dot_general x9 -> x0, matrix products: 10 us -> none  [the longest x8 8.41 us: dot(): lax.dot_general(left, right, dims, preferred_element_type=jnp.float32)]
    unnamed x29 -> x28, local copies, waits for them, and re-layouts: 5.4 us -> 8.61 us
  transfers between devices with their start and end apart: 6 -> 9, of which waited for: 4 -> 1; matrix products, arithmetic and copies ran while one was open for 5% -> 2% of each run, Pallas kernels for 1% -> 7%
where the time goes in v2:
time: 252 us; the launch traced here: 248 us
  starting transfers between devices  97.7 us (39%)
  blocking collectives  95 us (38%)
  Pallas kernels  22.9 us (9%)
  between operations  14.9 us (6%)
  local copies, waits for them, and re-layouts  12.7 us (5%)
  waiting for transfers between devices  2.6 us (1%)
    all_to_all x5, starting transfers between devices, exchange(): lax.all_to_all(array, axis, split_axis=0, concat_axis=0, tiled=True, axis...  75.2 us
    all_gather x2, blocking collectives, gather_far(): return lax.all_gather(piece, 'dp', axis=0, axis_index_groups=FAR)  60.6 us
    all_gather x2, blocking collectives, gather_near(): return lax.all_gather(piece, 'dp', axis=0, axis_index_groups=NEAR)  34.5 us
    pallas_call x9, Pallas kernels, call(): pl.pallas_call(body, out_shape=out_shape, in_specs=specs + [pl.BlockSpec(...  22.9 us
    ppermute x3, starting transfers between devices, send_far(): return lax.ppermute(piece, 'dp', pairs)  22.5 us
    unnamed x28, local copies, waits for them, and re-layouts  8.61 us
  transfers between devices with their start and end apart: 9, of which 1 were waited for; matrix products, arithmetic and copies ran while one was open for 2% of the time, Pallas kernels for 7%

profile of v2, /device:TPU:24, one launch (start us, length us, event | category | flops | bytes accessed | tf_op | source)
XLA Modules:
  0.0 248.3 jit_solution(8806193203200494031)
XLA Ops:
  7.2 0.8 copy-done.5
  8.0 0.7 copy-done.8
  8.7 1.3 dispatch.1
  10.0 9.3 %all-to-all-start.4 = ((bf16[32,16,128]{2,1,0:T(8,128)(2,1)}), bf16[32,16,128]{2,1,0:T(8,128)(2,1)S(1)}, u32[]{:S(2)}, u32[]{:S(2)}) async-start(bf16[32,16,128]{2,1,0:T(8,128)(2,1)} %get-tuple-element.71), calls=%async_computation.4 | async-start | bytes 262144 | tf_op jit(solution)/shard_map/all_to_all | solution.py:352
  19.3 0.0 copy-start
  19.3 1.1 copy-done
  20.4 1.1 copy-done.1
  21.4 1.1 copy-done.2
  22.5 0.7 copy-done.6
  23.2 0.7 copy-done.7
  24.0 6.7 %pack.1 = (bf16[16,456,128]{2,1,0:T(8,128)(2,1)}, s32[224,1]{1,0:T(8,128)S(1)}, s32[224,1]{1,0:T(8,128)S(1)}, s32[224,1]{1,0:T(8,128)S(1)}, s32[224,1]{1,0:T(8,128)}) custom-call(s32[1]{0:T(128)} %bitcast.7.refs_0_, s32[28,128]{1,0:T(8,128)S(1)} %bitcast.57, s32[28,128]{1,0:T(8,128)S(1)} %bitcast.58, bf16[304,1024]{1,0:T(8,128)(2,1)S(1)} %bitcast.53, ...), custom_call_target="tpu_custom_call" | custom-call | bytes 1024 | tf_op jit(solution)/shard_map/pack/pallas_call | solution.py:313
  30.7 0.6 copy-done.3
  31.4 0.0 all-to-all-done.4
  31.4 4.1 %all-to-all-start.5 = ((bf16[4,4,456,128]{3,2,1,0:T(8,128)(2,1)}), bf16[4,4,456,128]{3,2,1,0:T(8,128)(2,1)S(1)}, u32[]{:S(2)}, u32[]{:S(2)}) async-start(bf16[4,4,456,128]{3,2,1,0:T(8,128)(2,1)} %bitcast.19), calls=%async_computation.5 | async-start | bytes 3735552 | tf_op jit(solution)/shard_map/all_to_all | solution.py:352
  35.5 35.9 %all-gather.5 = bf16[2944,128]{1,0:T(8,128)(2,1)S(1)} all-gather(bf16[736,128]{1,0:T(8,128)(2,1)S(1)} %pad_maximum_fusion.4), channel_id=7, replica_groups={{0,4,8,12},{1,5,9,13},{2,6,10,14},{3,7,11,15},{16,20,24,28},{17,21,25,2..., dimensions={0}, use_global_device_ids=true | all-gather | bytes 942080 | tf_op jit(solution)/shard_map/all_gather | solution.py:38
  71.4 0.0 all-to-all-done.5
  71.4 0.9 slice.41
  72.3 0.0 all-gather.9.cloned.1.call-update
  72.5 0.9 copy.26
  73.3 5.8 %all-to-all-start.6 = ((bf16[4,4,152,128]{3,2,1,0:T(8,128)(2,1)}), bf16[4,4,152,128]{3,2,1,0:T(8,128)(2,1)S(1)}, u32[]{:S(2)}, u32[]{:S(2)}) async-start(bf16[4,4,152,128]{3,2,1,0:T(8,128)(2,1)} %copy.26), calls=%async_computation.6 | async-start | bytes 1245184 | tf_op jit(solution)/shard_map/all_to_all | solution.py:352
  79.2 0.1 slice_bitcast_fusion
  79.3 0.7 pad_maximum_fusion.1
  80.0 8.0 %collective-permute-start = (bf16[4,304,128]{2,1,0:T(8,128)(2,1)}, bf16[4,304,128]{2,1,0:T(8,128)(2,1)}, u32[]{:S(2)}, u32[]{:S(2)}) collective-permute-start(bf16[4,304,128]{2,1,0:T(8,128)(2,1)} %pad_maximum_fusion.1), channel_id=1, source_target_pairs={{0,4},{1,5},{2,6},{3,7},{4,8},{5,9},{6,10},{7,11},{8,12},{9,13},{1... | collective-permute-start | bytes 933896 | tf_op jit(solution)/shard_map/ppermute | solution.py:56
  88.0 0.7 pad_maximum_fusion.2
  88.7 7.3 %collective-permute-start.1 = (bf16[4,304,128]{2,1,0:T(8,128)(2,1)}, bf16[4,304,128]{2,1,0:T(8,128)(2,1)}, u32[]{:S(2)}, u32[]{:S(2)}) collective-permute-start(bf16[4,304,128]{2,1,0:T(8,128)(2,1)} %pad_maximum_fusion.2), channel_id=1, source_target_pairs={{0,8},{1,9},{2,10},{3,11},{4,12},{5,13},{6,14},{7,15},{8,0},{9,1},... | collective-permute-start | bytes 933896 | tf_op jit(solution)/shard_map/ppermute | solution.py:56
  96.0 0.7 pad_maximum_fusion.3
  96.7 7.3 %collective-permute-start.2 = (bf16[4,304,128]{2,1,0:T(8,128)(2,1)}, bf16[4,304,128]{2,1,0:T(8,128)(2,1)}, u32[]{:S(2)}, u32[]{:S(2)}) collective-permute-start(bf16[4,304,128]{2,1,0:T(8,128)(2,1)} %pad_maximum_fusion.3), channel_id=1, source_target_pairs={{0,12},{1,13},{2,14},{3,15},{4,0},{5,1},{6,2},{7,3},{8,4},{9,5},{1... | collective-permute-start | bytes 933896 | tf_op jit(solution)/shard_map/ppermute | solution.py:56
  104.0 1.2 slice.39
  105.9 1.0 slice.40
  106.9 0.0 all-to-all-done.6
  106.9 1.7 unpack.1.refs_1_
  108.6 2.6 %all-gather.9.cloned.1.call-done = bf16[16,512,128]{2,1,0:T(8,128)(2,1)} async-done(((bf16[4,512,128]{2,1,0:T(8,128)(2,1)}), bf16[16,512,128]{2,1,0:T(8,128)(2,1)}) %all-gather.9.cloned.1.call-update) | async-done | bytes 2097168 | tf_op jit(solution)/shard_map/all_gather | solution.py:42
  111.2 123.7 %conditional.1 = (bf16[224,128]{1,0:T(8,128)(2,1)S(1)}, f32[224,1024]{1,0:T(8,128)S(1)}) conditional(s32[]{:T(128)} %bitcast.6, (bf16[4,224,128]{2,1,0:T(8,128)(2,1)S(1)}, s32[224,1]{1,0:T(8,128)S(1)}, f32[4,128]{1,0:T(4,128)S(1)}, s32[4,128]{1,0:T(4,128)S(1)}, bf16[4,4,512,128]{3,2,1,0:T(8,128)(2,1)}, /*index=5*/bf16[224,1024]{1,0:T(8,128)(2,1)}, ...), branch_computations={%region_0.0_spmd, %region_1.0_spmd} | conditional | bytes 6980204 | solution.py:440
  111.2 4.3 %forward.3 = (bf16[2,512,1024]{2,1,0:T(8,128)(2,1)S(1)}, bf16[32,32,224]{2,1,0:T(8,128)(2,1)}) custom-call(bf16[4,4,512,128]{3,2,1,0:T(8,128)(2,1)} %get-tuple-element.43.refs_0_, bf16[224,1024]{1,0:T(8,128)(2,1)} %get-tuple-element.44.refs_1_), custom_call_target="tpu_custom_call" | custom-call | bytes 1024 | tf_op jit(solution)/shard_map/cond/branch_1_fun/forward/pallas_call | solution.py:313
  115.4 48.4 %all-to-all-start = ((bf16[32,32,224]{2,1,0:T(8,128)(2,1)}), bf16[32,32,224]{2,1,0:T(8,128)(2,1)S(1)}, u32[]{:S(2)}, u32[]{:S(2)}) async-start(bf16[32,32,224]{2,1,0:T(8,128)(2,1)} %get-tuple-element.45), calls=%async_computation | async-start | bytes 1048576 | tf_op jit(solution)/shard_map/cond/branch_1_fun/all_to_all | solution.py:352
  163.8 19.8 %all-gather.2 = bf16[16,224,128]{2,1,0:T(8,128)(2,1)S(1)} all-gather(bf16[4,224,128]{2,1,0:T(8,128)(2,1)S(1)} %get-tuple-element.39), channel_id=4, replica_groups={{0,1,2,3},{4,5,6,7},{8,9,10,11},{12,13,14,15},{16,17,18,19},{20,21,22,2..., dimensions={0}, use_global_device_ids=true | all-gather | bytes 1146880 | tf_op jit(solution)/shard_map/cond/branch_1_fun/all_gather | solution.py:42
  183.6 2.5 scale.3
  186.0 0.0 all-to-all-done.refs_0_
  186.1 7.7 %all-to-all-start.1 = ((bf16[32,32,224]{2,1,0:T(8,128)(2,1)}), bf16[32,32,224]{2,1,0:T(8,128)(2,1)S(1)}, u32[]{:S(2)}, u32[]{:S(2)}) async-start(bf16[32,32,224]{2,1,0:T(8,128)(2,1)} %scale.3), calls=%async_computation.1 | async-start | bytes 1048576 | tf_op jit(solution)/shard_map/cond/branch_1_fun/all_to_all | solution.py:352
  193.8 0.4 combine.3
  194.2 24.7 %all-gather.3 = bf16[896,128]{1,0:T(8,128)(2,1)S(1)} all-gather(bf16[224,128]{1,0:T(8,128)(2,1)S(1)} %combine.3), channel_id=5, replica_groups={{0,4,8,12},{1,5,9,13},{2,6,10,14},{3,7,11,15},{16,20,24,28},{17,21,25,2..., dimensions={0}, use_global_device_ids=true | all-gather | bytes 286720 | tf_op jit(solution)/shard_map/cond/branch_1_fun/all_gather | solution.py:38
  218.9 14.7 %all-gather.4 = bf16[16,224,128]{2,1,0:T(8,128)(2,1)S(1)} all-gather(bf16[4,224,128]{2,1,0:T(8,128)(2,1)S(1)} %bitcast.65), channel_id=6, replica_groups={{0,1,2,3},{4,5,6,7},{8,9,10,11},{12,13,14,15},{16,17,18,19},{20,21,22,2..., dimensions={0}, use_global_device_ids=true | all-gather | bytes 1146880 | tf_op jit(solution)/shard_map/cond/branch_1_fun/all_gather | solution.py:42
  233.6 0.7 pick.3
  234.3 0.7 gradient.3
  235.0 0.0 copy-start.14
  235.0 0.9 copy-done.9
  235.9 0.9 copy-done.4
  236.8 4.7 %update.1 = (bf16[224,1024]{1,0:T(8,128)(2,1)}, bf16[224,1024]{1,0:T(8,128)(2,1)}, bf16[224,1024]{1,0:T(8,128)(2,1)}) custom-call(f32[224,1024]{1,0:T(8,128)} %copy-done.9, bf16[224,1024]{1,0:T(8,128)(2,1)} %unpack.1.refs_1_, bf16[4,304,128]{2,1,0:T(8,128)(2,1)S(1)} %pad_maximum_fusion.refs_2_, bf16[4,304,128]{2,1,0:T(8,128)(2,1)} %collective-permute-done.refs_3_, ...), custom_call_target="tpu_custom_call" | custom-call | bytes 1024 | tf_op jit(solution)/shard_map/update/pallas_call | solution.py:313
  (29 shorter events, 0.2 us)
Async XLA Ops:
  7.2 0.8 copy-start.5
  8.0 0.7 copy-start.8
  10.0 21.3 %all-to-all-start.4 = ((bf16[32,16,128]{2,1,0:T(8,128)(2,1)}), bf16[32,16,128]{2,1,0:T(8,128)(2,1)S(1)}, u32[]{:S(2)}, u32[]{:S(2)}) async-start(bf16[32,16,128]{2,1,0:T(8,128)(2,1)} %get-tuple-element.71), calls=%async_computation.4 | async-start | bytes 262144 | tf_op jit(solution)/shard_map/all_to_all | solution.py:352
  19.3 1.1 copy-start
  20.4 1.1 copy-start.1
  21.4 1.1 copy-start.2
  22.5 0.7 copy-start.6
  23.2 0.7 copy-start.7
  30.7 0.7 copy-start.3
  31.4 4.1 %copy-start.13 = (bf16[128,224]{0,1:T(8,128)(2,1)S(1)}, bf16[128,224]{0,1:T(8,128)(2,1)}, u32[]{:S(2)}) copy-start(bf16[128,224]{0,1:T(8,128)(2,1)} %param.14) | copy-start | bytes 172036
  31.4 40.0 %all-to-all-start.5 = ((bf16[4,4,456,128]{3,2,1,0:T(8,128)(2,1)}), bf16[4,4,456,128]{3,2,1,0:T(8,128)(2,1)S(1)}, u32[]{:S(2)}, u32[]{:S(2)}) async-start(bf16[4,4,456,128]{3,2,1,0:T(8,128)(2,1)} %bitcast.19), calls=%async_computation.5 | async-start | bytes 3735552 | tf_op jit(solution)/shard_map/all_to_all | solution.py:352
  35.5 75.7 %all-gather.9.cloned.1.call-start = ((), (), s32[]{:S(2)}) async-start(), calls=%async_computation.7 | async-start | bytes 2621440 | tf_op jit(solution)/shard_map/all_gather | solution.py:42
  71.4 1.1 copy-start.10
  73.3 33.5 %all-to-all-start.6 = ((bf16[4,4,152,128]{3,2,1,0:T(8,128)(2,1)}), bf16[4,4,152,128]{3,2,1,0:T(8,128)(2,1)S(1)}, u32[]{:S(2)}, u32[]{:S(2)}) async-start(bf16[4,4,152,128]{3,2,1,0:T(8,128)(2,1)} %copy.26), calls=%async_computation.6 | async-start | bytes 1245184 | tf_op jit(solution)/shard_map/all_to_all | solution.py:352
  80.0 31.2 %copy-start.15 = (f32[128,4]{0,1:T(4,128)S(1)}, f32[128,4]{0,1:T(4,128)}, u32[]{:S(2)}) copy-start(f32[128,4]{0,1:T(4,128)} %param.13) | copy-start | bytes 6148
  80.0 155.0 %collective-permute-start = (bf16[4,304,128]{2,1,0:T(8,128)(2,1)}, bf16[4,304,128]{2,1,0:T(8,128)(2,1)}, u32[]{:S(2)}, u32[]{:S(2)}) collective-permute-start(bf16[4,304,128]{2,1,0:T(8,128)(2,1)} %pad_maximum_fusion.1), channel_id=1, source_target_pairs={{0,4},{1,5},{2,6},{3,7},{4,8},{5,9},{6,10},{7,11},{8,12},{9,13},{1... | collective-permute-start | bytes 933896 | tf_op jit(solution)/shard_map/ppermute | solution.py:56
  88.7 146.3 %collective-permute-start.1 = (bf16[4,304,128]{2,1,0:T(8,128)(2,1)}, bf16[4,304,128]{2,1,0:T(8,128)(2,1)}, u32[]{:S(2)}, u32[]{:S(2)}) collective-permute-start(bf16[4,304,128]{2,1,0:T(8,128)(2,1)} %pad_maximum_fusion.2), channel_id=1, source_target_pairs={{0,8},{1,9},{2,10},{3,11},{4,12},{5,13},{6,14},{7,15},{8,0},{9,1},... | collective-permute-start | bytes 933896 | tf_op jit(solution)/shard_map/ppermute | solution.py:56
  96.7 138.2 %collective-permute-start.2 = (bf16[4,304,128]{2,1,0:T(8,128)(2,1)}, bf16[4,304,128]{2,1,0:T(8,128)(2,1)}, u32[]{:S(2)}, u32[]{:S(2)}) collective-permute-start(bf16[4,304,128]{2,1,0:T(8,128)(2,1)} %pad_maximum_fusion.3), channel_id=1, source_target_pairs={{0,12},{1,13},{2,14},{3,15},{4,0},{5,1},{6,2},{7,3},{8,4},{9,5},{1... | collective-permute-start | bytes 933896 | tf_op jit(solution)/shard_map/ppermute | solution.py:56
  115.4 70.6 %all-to-all-start = ((bf16[32,32,224]{2,1,0:T(8,128)(2,1)}), bf16[32,32,224]{2,1,0:T(8,128)(2,1)S(1)}, u32[]{:S(2)}, u32[]{:S(2)}) async-start(bf16[32,32,224]{2,1,0:T(8,128)(2,1)} %get-tuple-element.45), calls=%async_computation | async-start | bytes 1048576 | tf_op jit(solution)/shard_map/cond/branch_1_fun/all_to_all | solution.py:352
  186.1 48.2 %all-to-all-start.1 = ((bf16[32,32,224]{2,1,0:T(8,128)(2,1)}), bf16[32,32,224]{2,1,0:T(8,128)(2,1)S(1)}, u32[]{:S(2)}, u32[]{:S(2)}) async-start(bf16[32,32,224]{2,1,0:T(8,128)(2,1)} %scale.3), calls=%async_computation.1 | async-start | bytes 1048576 | tf_op jit(solution)/shard_map/cond/branch_1_fun/all_to_all | solution.py:352
  193.7 39.8 %copy-start.12 = (s32[224,1]{1,0:T(8,128)S(1)}, s32[224,1]{1,0:T(8,128)}, u32[]{:S(2)}) copy-start(s32[224,1]{1,0:T(8,128)} %get-tuple-element.47.refs_1_) | copy-start | bytes 2692 | tf_op jit(solution)/shard_map/cond
  234.9 0.9 copy-start.9
  235.0 6.5 %copy-start.14 = (bf16[224,128]{1,0:T(8,128)(2,1)}, bf16[224,128]{1,0:T(8,128)(2,1)S(1)}, u32[]{:S(2)}) copy-start(bf16[224,128]{1,0:T(8,128)(2,1)S(1)} %get-tuple-element.80) | copy-start | bytes 172036
  235.9 0.9 copy-start.4
Sparse Core Ops, SparseCore 0:
  72.5 38.6 all-gather.8

commit v3 on v2

--- a/solution.py
+++ b/solution.py
@@ -14,6 +14,7 @@
 bias_two = 1.0 - 0.95**50 * 0.95**50
 
 RING = 4
+OLD_FAR = 3 * RING // 4
 NEAR = [[far * RING + near for near in range(RING)] for far in range(RING)]
 FAR = [[far * RING + near for far in range(RING)] for near in range(RING)]
 
@@ -22,6 +23,7 @@
 ROWS = 16
 
 VMEM_BYTES = 48 * 1024 * 1024
+PACK_VMEM_BYTES = 60 * 1024 * 1024
 CONTRACT_LAST = (((1,), (1,)), ((), ()))
 CONTRACT_FIRST = (((0,), (0,)), ((), ()))
 
@@ -40,17 +42,12 @@
 
 def gather_near(piece):
     return lax.all_gather(piece, "dp", axis=0, axis_index_groups=NEAR)
-
-
-def gather_whole(piece):
-    every = lax.all_gather(piece, "dp", axis=0)
-    return every.reshape(RING, RING, *piece.shape).swapaxes(0, 1)
 
 
 def send_far(piece, step):
     pairs = [
         (far * RING + near, (far + step) % RING * RING + near)
-        for far in range(RING)
+        for far in range(OLD_FAR)
         for near in range(RING)
     ]
     return lax.ppermute(piece, "dp", pairs)
@@ -66,14 +63,15 @@
     return jnp.sum(jnp.where(same, column, 0), axis=0, keepdims=True)
 
 
-def pick(blocks_ref, wanted):
-    near, far, width, tokens = blocks_ref.shape
+def pick(blocks_ref, wanted, first=0):
+    near, far, every, tokens = blocks_ref.shape
+    width = every - first
     column = iota((wanted.shape[0], width), 1)
     total = jnp.zeros((wanted.shape[0], tokens), jnp.float32)
     for x in range(near):
         for z in range(far):
             hot = (column + (z * near + x) * width == wanted).astype(jnp.bfloat16)
-            total += dot(hot, blocks_ref[x, z])
+            total += dot(hot, blocks_ref[x, z, first:, :])
     return total
 
 
@@ -112,14 +110,21 @@
 
 
 def scale_kernel(blocks_ref, wanted_ref, gates_ref, slot_ref, packed_ref):
-    experts, cap, width = packed_ref.shape
-    top = gates_ref.shape[0]
-    chosen = pick(blocks_ref, wanted_ref[...])
+    experts, lines, lanes = packed_ref.shape
+    cap, width = lines // 2, wanted_ref.shape[0]
+    top, tokens = gates_ref.shape
+    chosen = pick(blocks_ref, wanted_ref[...], blocks_ref.shape[2] - width)
     scaled = jnp.concatenate(
         [(gates_ref[k : k + 1, :] * chosen).astype(jnp.bfloat16) for k in range(top)], axis=1
     )
     hot = slot_hot(slot_ref, experts * cap)
-    packed_ref[...] = dot(hot, scaled, CONTRACT_LAST).astype(jnp.bfloat16).reshape(packed_ref.shape)
+    short = 2 * lanes - width
+    scaled = jnp.concatenate([scaled, jnp.zeros((short, top * tokens), jnp.bfloat16)], axis=0)
+    packed = dot(hot, scaled, CONTRACT_LAST).astype(jnp.bfloat16)
+    for c in range(2):
+        packed_ref[:, c * cap : (c + 1) * cap, :] = packed[:, c * lanes : (c + 1) * lanes].reshape(
+            experts, cap, lanes
+        )
 
 
 def tables(me, old_ref, new_ref, old_rows, width, cap):
@@ -128,7 +133,6 @@
     leaving = jnp.zeros((old_rows, lanes), jnp.int32)
     origin = jnp.zeros((width, lanes), jnp.int32)
     model = jnp.zeros((width, lanes), jnp.int32)
-    own = jnp.zeros((width, lanes), jnp.int32)
     for i in range(blocks):
         old, new = old_ref[i : i + 1, :], new_ref[i : i + 1, :]
         number = iota((1, lanes), 1) + i * lanes
@@ -137,10 +141,18 @@
         held = new - me * width == row
         origin += jnp.where(held, old, 0)
         model += jnp.where(held, number, 0)
-        own += jnp.where(number - me * width == row, new, 0)
-    leaving, origin, model, own = [
-        jnp.sum(part, axis=1, keepdims=True) for part in (leaving, origin, model, own)
+    leaving, origin, model = [
+        jnp.sum(part, axis=1, keepdims=True) for part in (leaving, origin, model)
     ]
+    mine = RING * width // lanes
+    same = iota((lanes, lanes), 0) == iota((lanes, lanes), 1)
+    own = jnp.concatenate(
+        [
+            jnp.sum(jnp.where(same, old_ref[pl.ds(far * mine + i, 1), :], 0), axis=1, keepdims=True)
+            for i in range(mine)
+        ],
+        axis=0,
+    )
     leaving_row = to_row(leaving)
     target, target_row = (leaving - 1) // width, (leaving_row - 1) // width
     size = (old_rows, old_rows)
@@ -150,18 +162,16 @@
         keepdims=True,
     )
     step = (target_row // RING - far + RING) % RING
-    first = target_row % RING * RING
-    send = jnp.where(leaving_row > 0, (first + target_row // RING) * cap + rank, -1)
-    send_step = jnp.where(leaving_row > 0, (first + step) * cap + rank, -1)
+    send = (target_row % RING * RING + step) * cap + rank
+    send = jnp.where(leaving_row > 0, send, -1)
     origin_row = to_row(origin)
     owner, owner_row = origin // old_rows, origin_row // old_rows
     rank = jnp.sum(
         ((owner == owner_row) & (origin_row < origin)).astype(jnp.int32), axis=1, keepdims=True
     )
     step = (far - owner // RING + RING) % RING
-    recv = owner * cap + rank
-    recv_step = (step * RING + owner % RING) * cap + rank
-    return send, send_step, recv, recv_step, model, own
+    recv = (step * RING + owner % RING) * cap + rank
+    return send, recv, model, own
 
 
 def pack_lines(source, slot, devices, cap):
@@ -183,20 +193,20 @@
 
 
 def pack_kernel(me_ref, old_ref, new_ref, *refs):
-    sources, (out_ref, recv_ref, recv_step_ref, model_ref, own_ref, held, sems) = refs[:3], refs[3:]
+    sources, (out_ref, recv_ref, model_ref, own_ref, held, sems) = refs[:3], refs[3:]
     copies = [pltpu.make_async_copy(source, held.at[i], sems.at[i]) for i, source in enumerate(sources)]
     for copy in copies:
         copy.start()
     devices, lines, _ = out_ref.shape
     cap = lines // (CHUNKS * len(sources))
-    send, send_step, recv_ref[...], recv_step_ref[...], model_ref[...], own_ref[...] = tables(
+    send, recv_ref[...], model_ref[...], own_ref[...] = tables(
         me_ref[0], old_ref, new_ref, held.shape[1], recv_ref.shape[0], cap
     )
     for copy in copies:
         copy.wait()
     place, tails = 0, []
     for number in range(len(sources)):
-        mains, tail = pack_lines(held[number], send_step if number else send, devices, cap)
+        mains, tail = pack_lines(held[number], send, devices, cap)
         for main in mains:
             out_ref[:, place : place + ROWS, :] = main.astype(jnp.bfloat16)
             place += ROWS
@@ -229,68 +239,102 @@
         return dot(self.main, jnp.concatenate(rows, axis=0)) + dot(self.tail, rest)
 
 
-def unpack_kernel(got_ref, recv_ref, weight_ref):
-    arrived = Arrived([got_ref], recv_ref[...], 1)
-    for c in range(CHUNKS):
-        weight_ref[:, c * LANES : (c + 1) * LANES] = arrived.piece(0, c).astype(jnp.bfloat16)
-
-
-def forward_kernel(acts_ref, weight_ref, rows_ref, out_ref):
-    near, far, rows, lanes = acts_ref.shape
+def forward_kernel(acts_ref, weight_ref, scaled_ref, rows_ref, out_ref):
+    near, far, _, lanes = acts_ref.shape
+    rows = rows_ref.shape[1]
     half = lanes // 2
     source, target = iota((2 * lanes, lanes), 0), iota((2 * lanes, lanes), 1)
     picked = jnp.where(target < half, target, target + half)
     shuffles = [(source == picked + side * half).astype(jnp.bfloat16) for side in range(2)]
     for z in range(far):
         for x in range(0, near, 2):
-            pair = jnp.concatenate([acts_ref[x, z], acts_ref[x + 1, z]], axis=1)
+            pair = jnp.concatenate([acts_ref[x, z, :rows, :], acts_ref[x + 1, z, :rows, :]], axis=1)
             first = (z * near + x) * half
             for side in range(2):
                 rows_ref[side, :, first : first + lanes] = dot(pair, shuffles[side]).astype(
                     jnp.bfloat16
                 )
-    blocks, slots, width = out_ref.shape
+    blocks, lines, _ = scaled_ref.shape
+    part = lines // 4
+    out_ref[:, 5 * part :, :] = scaled_ref[...]
+    columns, hidden = weight_ref.shape
+    short = 5 * lanes // 2 - columns
+    weight = jnp.concatenate([weight_ref[...], jnp.zeros((short, hidden), jnp.bfloat16)], axis=0)
+    last = []
     for side in range(2):
-        result = dot(rows_ref[side], weight_ref[...], CONTRACT_LAST).astype(jnp.bfloat16)
-        out_ref[:, side * (slots // 2) : (side + 1) * (slots // 2), :] = result.reshape(
-            blocks, slots // 2, width
-        )
+        result = dot(rows_ref[side], weight, CONTRACT_LAST).astype(jnp.bfloat16)
+        for c in range(2):
+            first = (2 * c + side) * part
+            out_ref[:, first : first + part, :] = result[:, c * lanes : (c + 1) * lanes].reshape(
+                blocks, part, lanes
+            )
+        last.append(result[:, 2 * lanes :])
+    out_ref[:, 4 * part : 5 * part, :] = jnp.concatenate(last, axis=1).reshape(blocks, part, lanes)
 
 
 def combine_kernel(returned_ref, gates_ref, slot_ref, out_ref):
-    experts, cap, width = returned_ref.shape
+    experts, lines, lanes = returned_ref.shape
+    part = lines // 9
     top, tokens = gates_ref.shape
-    rows = returned_ref[...].reshape(experts * cap, width)
-    each = dot(rows, slot_hot(slot_ref, experts * cap), CONTRACT_FIRST)
-    total = jnp.zeros((width, tokens), jnp.float32)
-    for k in range(top):
-        total += gates_ref[k : k + 1, :] * each[:, k * tokens : (k + 1) * tokens]
-    out_ref[...] = total.astype(jnp.bfloat16)
-
-
-def pick_kernel(blocks_ref, wanted_ref, out_ref):
-    out_ref[...] = pick(blocks_ref, wanted_ref[...]).astype(jnp.bfloat16)
-
-
-def gradient_kernel(rows_ref, scaled_ref, out_ref):
-    blocks, slots, width = scaled_ref.shape
-    half = slots // 2
-    total = jnp.zeros(out_ref.shape, jnp.float32)
+    hot = slot_hot(slot_ref, experts * 2 * part).reshape(experts, 2 * part, top * tokens)
+    each = [0.0, 0.0, 0.0]
     for side in range(2):
-        scaled = scaled_ref[:, side * half : (side + 1) * half, :].reshape(blocks * half, width)
-        total += dot(scaled, rows_ref[side], CONTRACT_FIRST)
-    out_ref[...] = total
-
-
-def update_kernel(gradient_ref, weight_ref, *refs):
+        mine = hot[:, side * part : (side + 1) * part, :].reshape(experts * part, top * tokens)
+        for c in range(3):
+            first = (2 * c + side) * part if c < 2 else 4 * part
+            rows = returned_ref[:, first : first + part, :].reshape(experts * part, lanes)
+            if c == 2:
+                rows = rows[:, side * (lanes // 2) : (side + 1) * (lanes // 2)]
+            each[c] += dot(rows, mine, CONTRACT_FIRST)
+    first = 0
+    for piece in each:
+        total = jnp.zeros((piece.shape[0], tokens), jnp.float32)
+        for k in range(top):
+            total += gates_ref[k : k + 1, :] * piece[:, k * tokens : (k + 1) * tokens]
+        count = min(piece.shape[0], out_ref.shape[0] - first)
+        out_ref[first : first + count, :] = total[:count].astype(jnp.bfloat16)
+        first += count
+
+
+def spread_kernel(me_ref, blocks_ref, own_ref, out_ref):
+    far, width, tokens = blocks_ref.shape
+    far = OLD_FAR
+    near = me_ref[0] % RING
+    column = iota((own_ref.shape[0], far * width), 1)
+    column = (column // width * RING + near) * width + column % width
+    hot = (column == own_ref[...]).astype(jnp.bfloat16)
+    rows = dot(hot, blocks_ref[:far].reshape(far * width, tokens))
+    out_ref[...] = rows.astype(jnp.bfloat16).reshape(out_ref.shape)
+
+
+def sum_kernel(parts_ref, out_ref):
+    out_ref[...] = jnp.sum(parts_ref[...].astype(jnp.float32), axis=0).astype(jnp.bfloat16)
+
+
+def gradient_kernel(rows_ref, returned_ref, out_ref):
+    blocks, lines, lanes = returned_ref.shape
+    part = lines // 9
+    total = 0.0
+    for side in range(2):
+        scaled = [
+            returned_ref[:, (5 + 2 * c + side) * part : (6 + 2 * c + side) * part, :].reshape(
+                blocks * part, lanes
+            )
+            for c in range(2)
+        ]
+        total += dot(jnp.concatenate(scaled, axis=1), rows_ref[side], CONTRACT_FIRST)
+    out_ref[...] = total[: out_ref.shape[0]]
+
+
+def update_kernel(gradient_ref, *refs):
     recv_ref, w_ref, m_ref, v_ref = refs[RING:]
-    arrived = Arrived(refs[:RING], recv_ref[...], 2)
+    arrived = Arrived(refs[:RING], recv_ref[...], 3)
     for c in range(CHUNKS):
         piece = slice(c * LANES, (c + 1) * LANES)
         gradient = gradient_ref[:, piece]
-        weight = weight_ref[:, piece].astype(jnp.float32)
-        one_next = beta_one * arrived.piece(0, c) + (1.0 - beta_one) * gradient
-        two_next = beta_two * arrived.piece(1, c) + (1.0 - beta_two) * gradient * gradient
+        weight = arrived.piece(0, c)
+        one_next = beta_one * arrived.piece(1, c) + (1.0 - beta_one) * gradient
+        two_next = beta_two * arrived.piece(2, c) + (1.0 - beta_two) * gradient * gradient
         update = (
             one_next / bias_one / (jnp.sqrt(two_next / bias_two) + adam_eps)
             + weight_decay * weight
@@ -300,7 +344,7 @@
         v_ref[:, piece] = two_next.astype(jnp.bfloat16)
 
 
-def call(kernel, name, out_shape, *args, flops=0, scalars=0, apart=(), scratch=(), order=()):
+def call(kernel, name, out_shape, *args, flops=0, scalars=0, apart=(), scratch=(), order=(), vmem=VMEM_BYTES):
     several = isinstance(out_shape, tuple)
     count = len(args)
 
@@ -316,7 +360,7 @@
         in_specs=specs + [pl.BlockSpec(memory_space=pl.ANY)] * len(order),
         out_specs=tuple(whole() for _ in out_shape) if several else whole(),
         scratch_shapes=scratch,
-        compiler_params=pltpu.CompilerParams(vmem_limit_bytes=VMEM_BYTES),
+        compiler_params=pltpu.CompilerParams(vmem_limit_bytes=vmem),
         cost_estimate=pl.CostEstimate(flops=flops, bytes_accessed=1024, transcendentals=0),
         name=name,
     )(*args, *order)
@@ -363,20 +407,27 @@
     )
     arrived = exchange(packed, "expert")
 
+    device = me[None].astype(int32)
     lines = hidden // LANES * move_cap
     old_rows = weight_old.shape[1]
     column = shape(width, 1, dtype=int32)
-    sent, recv, recv_step, model, own = call(
+    sent, recv, model, own = call(
         pack_kernel,
         "pack",
-        (shape(n_data, 3 * lines, LANES), column, column, column, column),
-        me[None].astype(int32),
+        (
+            shape(n_data, 3 * lines, LANES),
+            column,
+            column,
+            shape(RING * width, 1, dtype=int32),
+        ),
+        device,
         old_place.reshape(-1, LANES),
         new_place.reshape(-1, LANES),
         weight_old[0],
         first_old[0],
         second_old[0],
         scalars=1,
+        vmem=PACK_VMEM_BYTES,
         apart=(3, 4, 5),
         scratch=[pltpu.VMEM((3, old_rows, hidden), jnp.bfloat16), pltpu.SemaphoreType.DMA((3,))],
     )
@@ -385,79 +436,62 @@
 
     both = jnp.concatenate([arrived.reshape(rows, 2 * piece), cotangent.T], axis=0)
     both_far, state = lax.optimization_barrier((gather_far(both), state))
-    acts_all = gather_near(both_far[:, :rows])
-    cot_far = both_far[:, rows:]
+    both_all = gather_near(both_far)
     gates = gate_weights.T
 
-    block = ROWS * CHUNKS
-    rest = lines - block
-    weight_sent = jnp.concatenate(
-        [state[:, :, :block], state[:, :, 3 * block : 3 * block + rest]], axis=2
-    ).transpose(1, 0, 2, 3)
-    weight_got = exchange(weight_sent, "dp", FAR).reshape(n_data, lines, LANES)
-    weight_now = call(unpack_kernel, "unpack", shape(width, hidden), weight_got, recv)
-    moments_got = []
-    for step in range(RING):
-        moments = jnp.concatenate(
-            [state[:, step, block : 3 * block], state[:, step, 3 * block + rest :]], axis=1
-        )
-        moments_got.append(send_far(moments, step) if step else moments)
-
-    def tail(gather):
-        def run(acts_all, weight_now, cot_far, slot, gates, model, own):
+    scaled = call(
+        scale_kernel, "scale", shape(n_expert, 2 * cap, LANES), both_all, model, gates, slot
+    )
+
+    state_got = [send_far(state[:, step], step) if step else state[:, 0] for step in range(RING)]
+
+    def tail(forward_name):
+        def run(both_all, weight, scaled, slot, gates):
             rows_now, outputs = call(
                 forward_kernel,
-                "forward",
-                (shape(2, rows, hidden), shape(n_expert, cap, width)),
-                acts_all,
-                weight_now,
+                forward_name,
+                (shape(2, rows, hidden), shape(n_expert, 9 * cap // 2, LANES)),
+                both_all,
+                weight,
+                scaled,
             )
             returned = exchange(outputs, "expert")
-            scaled = call(
-                scale_kernel,
-                "scale",
-                shape(n_expert, cap, width),
-                gather_near(cot_far),
-                model,
-                gates,
-                slot,
-            )
-            scaled, returned = lax.optimization_barrier((scaled, returned))
-            scaled_got = exchange(scaled, "expert")
-            part = call(combine_kernel, "combine", shape(width, tok_rows), returned, gates, slot)
-            gradient = call(
-                gradient_kernel,
-                "gradient",
-                shape(width, hidden, dtype=jnp.float32),
-                rows_now,
-                scaled_got,
-            )
-            combined = call(pick_kernel, "pick", shape(width, tok_rows), gather(part), own)
-            return combined, gradient
+            part = call(combine_kernel, "combine", shape(old_rows, tok_rows), returned, gates, slot)
+            return rows_now, part, returned
 
         return run
 
-    combined, gradient = lax.cond(
+    rows_now, part, returned = lax.cond(
         new_place[0] >= 0,
-        tail(lambda part: gather_near(gather_far(part))),
-        tail(gather_whole),
-        acts_all,
-        weight_now,
-        cot_far,
+        tail("forward"),
+        tail("forward_too"),
+        both_all,
+        weight_old[0],
+        scaled,
         slot,
         gates,
-        model,
+    )
+    part, state_got = lax.optimization_barrier((part, state_got))
+    spread = call(
+        spread_kernel,
+        "spread",
+        shape(RING, width, tok_rows),
+        device,
+        gather_far(part),
         own,
-    )
-    combined = combined.T
+        scalars=1,
+    )
+    combined = call(sum_kernel, "sum", shape(width, tok_rows), exchange(spread, "dp", NEAR)).T
+    gradient = call(
+        gradient_kernel, "gradient", shape(width, hidden, dtype=jnp.float32), rows_now, returned
+    )
     new_weight, new_one, new_two = call(
         update_kernel,
         "update",
         (shape(width, hidden),) * 3,
         gradient,
-        weight_now,
-        *moments_got,
-        recv_step,
+        *state_got,
+        recv,
     )
     return (combined, new_weight[None], new_one[None], new_two[None])
 

time: 252 us -> 229 us (0.909)
  the two profiles are of different devices: /device:TPU:24 before, /device:TPU:90 now
where the time goes in v3:
time: 229 us; the launch traced here: 228 us
  blocking collectives  110 us (48%)
  waiting for transfers between devices  44.5 us (19%)
  starting transfers between devices  30.2 us (13%)
  Pallas kernels  24.3 us (11%)
  between operations  14.8 us (6%)
  local copies, waits for them, and re-layouts  3.87 us (2%)
    all_gather x2, blocking collectives, gather_far(): return lax.all_gather(piece, 'dp', axis=0, axis_index_groups=FAR)  69.8 us
    all_gather x1, waiting for transfers between devices, gather_near(): return lax.all_gather(piece, 'dp', axis=0, axis_index_groups=NEAR)  44.4 us
    all_to_all x1, blocking collectives, exchange(): lax.all_to_all(array, axis, split_axis=0, concat_axis=0, tiled=True, axis...  40.5 us
    pallas_call x9, Pallas kernels, call(): pl.pallas_call(body, out_shape=out_shape, in_specs=specs + [pl.BlockSpec(...  24.3 us
    all_to_all x3, starting transfers between devices, exchange(): lax.all_to_all(array, axis, split_axis=0, concat_axis=0, tiled=True, axis...  17.7 us
    ppermute x3, starting transfers between devices, send_far(): return lax.ppermute(piece, 'dp', pairs)  12.5 us
  transfers between devices with their start and end apart: 7, of which 1 were waited for; matrix products, arithmetic and copies ran while one was open for 1% of the time, Pallas kernels for 9%

profile of v3, /device:TPU:90, one launch (start us, length us, event | category | flops | bytes accessed | tf_op | source)
XLA Modules:
  0.0 228.4 jit_solution(11836086801481823388)
XLA Ops:
  7.2 0.0 copy-start.3
  7.2 0.8 copy-done.3
  8.0 0.0 copy-start.4
  8.0 0.7 copy-done.4
  8.7 1.3 dispatch.1
  10.0 8.1 %all-to-all-start.2 = ((bf16[32,16,128]{2,1,0:T(8,128)(2,1)}), bf16[32,16,128]{2,1,0:T(8,128)(2,1)S(1)}, u32[]{:S(2)}, u32[]{:S(2)}) async-start(bf16[32,16,128]{2,1,0:T(8,128)(2,1)} %get-tuple-element.60), calls=%async_computation.2 | async-start | bytes 262144 | tf_op jit(solution)/shard_map/all_to_all | solution.py:396
  18.1 6.6 %pack.1 = (bf16[16,456,128]{2,1,0:T(8,128)(2,1)}, s32[224,1]{1,0:T(8,128)}, s32[224,1]{1,0:T(8,128)}, s32[896,1]{1,0:T(8,128)}) custom-call(s32[1]{0:T(128)} %bitcast.refs_0_, s32[28,128]{1,0:T(8,128)} %bitcast.49, s32[28,128]{1,0:T(8,128)} %bitcast.50, bf16[304,1024]{1,0:T(8,128)(2,1)} %bitcast.36, bf16[304,1024]{1,0:T(8,128)(2,1)} %bitcast.41, ...), custom_call_target="tpu_custom_call" | custom-call | bytes 1024 | tf_op jit(solution)/shard_map/pack/pallas_call | solution.py:357
  24.7 0.0 all-to-all-done.2
  24.7 0.0 copy-start.7
  24.7 5.0 %all-to-all-start.3 = ((bf16[4,4,456,128]{3,2,1,0:T(8,128)(2,1)}), bf16[4,4,456,128]{3,2,1,0:T(8,128)(2,1)S(1)}, u32[]{:S(2)}, u32[]{:S(2)}) async-start(bf16[4,4,456,128]{3,2,1,0:T(8,128)(2,1)} %bitcast.40), calls=%async_computation.3 | async-start | bytes 3735552 | tf_op jit(solution)/shard_map/all_to_all | solution.py:396
  29.7 0.0 all-gather.5.cloned.1.call-start
  29.7 0.0 copy-done.7
  29.7 37.6 %all-gather = bf16[2944,128]{1,0:T(8,128)(2,1)} all-gather(bf16[736,128]{1,0:T(8,128)(2,1)S(1)} %pad_maximum_fusion), channel_id=2, replica_groups={{0,4,8,12},{1,5,9,13},{2,6,10,14},{3,7,11,15},{16,20,24,28},{17,21,25,2..., dimensions={0}, use_global_device_ids=true | all-gather | bytes 942080 | tf_op jit(solution)/shard_map/all_gather | solution.py:40
  67.3 0.0 all-to-all-done.3
  67.3 0.0 all-gather.5.cloned.1.call-update
  67.3 0.0 copy-start.2
  67.3 0.0 copy-start.8
  67.4 1.1 slice_bitcast_fusion
  68.5 0.0 copy-start.6
  68.5 3.9 %collective-permute-start.2 = (bf16[4,456,128]{2,1,0:T(8,128)(2,1)}, bf16[4,456,128]{2,1,0:T(8,128)(2,1)S(1)}, u32[]{:S(2)}, u32[]{:S(2)}) collective-permute-start(bf16[4,456,128]{2,1,0:T(8,128)(2,1)} %get-tuple-element.80), channel_id=1, source_target_pairs={{0,12},{1,13},{2,14},{3,15},{4,0},{5,1},{6,2},{7,3},{8,4},{9,5},{1... | collective-permute-start | bytes 1400840 | tf_op jit(solution)/shard_map/ppermute | solution.py:53
  72.4 7.2 %collective-permute-start.1 = (bf16[4,456,128]{2,1,0:T(8,128)(2,1)}, bf16[4,456,128]{2,1,0:T(8,128)(2,1)S(1)}, u32[]{:S(2)}, u32[]{:S(2)}) collective-permute-start(bf16[4,456,128]{2,1,0:T(8,128)(2,1)} %get-tuple-element.81), channel_id=1, source_target_pairs={{0,8},{1,9},{2,10},{3,11},{4,12},{5,13},{6,14},{7,15},{8,0},{9,1},... | collective-permute-start | bytes 1400840 | tf_op jit(solution)/shard_map/ppermute | solution.py:53
  79.6 1.4 collective-permute-start
  81.0 1.2 slice.15
  82.8 44.4 %all-gather.5.cloned.1.call-done = bf16[16,736,128]{2,1,0:T(8,128)(2,1)} async-done(((bf16[4,736,128]{2,1,0:T(8,128)(2,1)}), bf16[16,736,128]{2,1,0:T(8,128)(2,1)}) %all-gather.5.cloned.1.call-update) | async-done | bytes 3014672 | tf_op jit(solution)/shard_map/all_gather | solution.py:44
  127.3 0.0 copy-start.5
  127.3 0.0 copy-done.2
  127.3 0.0 copy-done.8
  127.3 3.6 %scale.1 = bf16[32,64,128]{2,1,0:T(8,128)(2,1)S(1)} custom-call(bf16[4,4,736,128]{3,2,1,0:T(8,128)(2,1)} %bitcast.33, s32[224,1]{1,0:T(8,128)S(1)} %copy-done.2, f32[4,128]{1,0:T(4,128)S(1)} %bitcast.46, s32[4,128]{1,0:T(4,128)S(1)} %get-tuple-element.65.refs_3_), custom_call_target="tpu_custom_call" | custom-call | bytes 1024 | tf_op jit(solution)/shard_map/scale/pallas_call | solution.py:357
  130.9 0.0 copy-done.6
  130.9 0.0 copy-done.5
  130.9 0.0 copy-start
  131.0 45.4 %conditional.1 = (bf16[2,512,1024]{2,1,0:T(8,128)(2,1)}, bf16[304,128]{1,0:T(8,128)(2,1)S(1)}, bf16[32,144,128]{2,1,0:T(8,128)(2,1)}) conditional(s32[]{:T(128)} %bitcast.1, (bf16[4,4,736,128]{3,2,1,0:T(8,128)(2,1)S(1)}, bf16[304,1024]{1,0:T(8,128)(2,1)S(1)}, bf16[32,64,128]{2,1,0:T(8,128)(2,1)S(1)}, f32[4,128]{1,0:T(4,128)S(1)}, ...), branch_computations={%region_0.0_spmd, %region_1.0_spmd} | conditional | bytes 2361368 | solution.py:464
  131.2 2.6 %forward.1 = (bf16[2,512,1024]{2,1,0:T(8,128)(2,1)}, bf16[32,144,128]{2,1,0:T(8,128)(2,1)S(1)}) custom-call(bf16[4,4,736,128]{3,2,1,0:T(8,128)(2,1)S(1)} %get-tuple-element.27.refs_0_, bf16[304,1024]{1,0:T(8,128)(2,1)S(1)} %get-tuple-element.28.refs_1_, bf16[32,64,128]{2,1,0:T(8,128)(2,1)S(1)} %get-tuple-element.29.refs_2_), custom_call_target="tpu_custom_call" | custom-call | bytes 1024 | tf_op jit(solution)/shard_map/cond/branch_1_fun/forward/pallas_call | solution.py:357
  133.8 40.5 %all_to_all.24.refs_0_ = bf16[32,144,128]{2,1,0:T(8,128)(2,1)} all-to-all(bf16[32,144,128]{2,1,0:T(8,128)(2,1)S(1)} %get-tuple-element.31), channel_id=1, replica_groups=mesh['expert'=32,'dp'=16] {'expert'}, dimensions={0} | all-to-all | bytes 2359296 | tf_op jit(solution)/shard_map/cond/branch_1_fun/all_to_all | solution.py:396
  174.2 1.9 combine.3
  176.4 0.0 collective-permute-done.2.refs_4_
  176.4 0.0 collective-permute-done.1.refs_3_
  176.4 0.0 collective-permute-done.refs_2_
  176.4 32.2 %all-gather.2 = bf16[1216,128]{1,0:T(8,128)(2,1)S(1)} all-gather(bf16[304,128]{1,0:T(8,128)(2,1)S(1)} %get-tuple-element.68), channel_id=4, replica_groups={{0,4,8,12},{1,5,9,13},{2,6,10,14},{3,7,11,15},{16,20,24,28},{17,21,25,2..., dimensions={0}, use_global_device_ids=true | all-gather | bytes 389120 | tf_op jit(solution)/shard_map/all_gather | solution.py:40
  208.6 0.0 copy-done
  208.6 1.4 spread.1
  210.0 4.6 %all-to-all-start.4 = ((bf16[4,224,128]{2,1,0:T(8,128)(2,1)}), bf16[4,224,128]{2,1,0:T(8,128)(2,1)S(1)}, u32[]{:S(2)}, u32[]{:S(2)}) async-start(bf16[4,224,128]{2,1,0:T(8,128)(2,1)} %spread.1), calls=%async_computation.4 | async-start | bytes 458752 | tf_op jit(solution)/shard_map/all_to_all | solution.py:396
  214.6 0.0 copy-start.1
  214.6 2.7 %gradient.1.refs_0_ = f32[224,1024]{1,0:T(8,128)S(1)} custom-call(bf16[2,512,1024]{2,1,0:T(8,128)(2,1)} %get-tuple-element.70.refs_0_, bf16[32,144,128]{2,1,0:T(8,128)(2,1)} %get-tuple-element.71.refs_1_), custom_call_target="tpu_custom_call" | custom-call | bytes 1024 | tf_op jit(solution)/shard_map/gradient/pallas_call | solution.py:357
  217.3 0.0 copy-done.1
  217.3 3.6 %update.1 = (bf16[224,1024]{1,0:T(8,128)(2,1)}, bf16[224,1024]{1,0:T(8,128)(2,1)}, bf16[224,1024]{1,0:T(8,128)(2,1)}) custom-call(f32[224,1024]{1,0:T(8,128)S(1)} %gradient.1.refs_0_, bf16[4,456,128]{2,1,0:T(8,128)(2,1)S(1)} %get-tuple-element.72.refs_1_, bf16[4,456,128]{2,1,0:T(8,128)(2,1)S(1)} %collective-permute-done.refs_2_, ...), custom_call_target="tpu_custom_call" | custom-call | bytes 1024 | tf_op jit(solution)/shard_map/update/pallas_call | solution.py:357
  220.8 0.0 all-to-all-done.4.refs_0_
  220.9 0.7 sum.1
  (1 shorter events, 0.0 us)
Async XLA Ops:
  7.2 0.8 copy-start.3
  8.0 0.7 copy-start.4
  10.0 14.7 %all-to-all-start.2 = ((bf16[32,16,128]{2,1,0:T(8,128)(2,1)}), bf16[32,16,128]{2,1,0:T(8,128)(2,1)S(1)}, u32[]{:S(2)}, u32[]{:S(2)}) async-start(bf16[32,16,128]{2,1,0:T(8,128)(2,1)} %get-tuple-element.60), calls=%async_computation.2 | async-start | bytes 262144 | tf_op jit(solution)/shard_map/all_to_all | solution.py:396
  24.7 5.0 %copy-start.7 = (bf16[128,224]{0,1:T(8,128)(2,1)S(1)}, bf16[128,224]{0,1:T(8,128)(2,1)}, u32[]{:S(2)}) copy-start(bf16[128,224]{0,1:T(8,128)(2,1)} %param.14) | copy-start | bytes 172036
  24.7 42.6 %all-to-all-start.3 = ((bf16[4,4,456,128]{3,2,1,0:T(8,128)(2,1)}), bf16[4,4,456,128]{3,2,1,0:T(8,128)(2,1)S(1)}, u32[]{:S(2)}, u32[]{:S(2)}) async-start(bf16[4,4,456,128]{3,2,1,0:T(8,128)(2,1)} %bitcast.40), calls=%async_computation.3 | async-start | bytes 3735552 | tf_op jit(solution)/shard_map/all_to_all | solution.py:396
  29.7 97.6 %all-gather.5.cloned.1.call-start = ((), (), s32[]{:S(2)}) async-start(), calls=%async_computation.5 | async-start | bytes 3768320 | tf_op jit(solution)/shard_map/all_gather | solution.py:44
  67.3 59.9 %copy-start.2 = (s32[224,1]{1,0:T(8,128)S(1)}, s32[224,1]{1,0:T(8,128)}, u32[]{:S(2)}) copy-start(s32[224,1]{1,0:T(8,128)} %get-tuple-element.64.refs_1_) | copy-start | bytes 2692
  67.3 59.9 %copy-start.8 = (f32[128,4]{0,1:T(4,128)S(1)}, f32[128,4]{0,1:T(4,128)}, u32[]{:S(2)}) copy-start(f32[128,4]{0,1:T(4,128)} %param.13) | copy-start | bytes 6148
  68.5 62.4 %copy-start.6 = (bf16[1,304,1024]{2,1,0:T(8,128)(2,1)S(1)}, bf16[1,304,1024]{2,1,0:T(8,128)(2,1)}, u32[]{:S(2)}) copy-start(bf16[1,304,1024]{2,1,0:T(8,128)(2,1)} %param.15) | copy-start | bytes 1867780
  68.5 107.9 %collective-permute-start.2 = (bf16[4,456,128]{2,1,0:T(8,128)(2,1)}, bf16[4,456,128]{2,1,0:T(8,128)(2,1)S(1)}, u32[]{:S(2)}, u32[]{:S(2)}) collective-permute-start(bf16[4,456,128]{2,1,0:T(8,128)(2,1)} %get-tuple-element.80), channel_id=1, source_target_pairs={{0,12},{1,13},{2,14},{3,15},{4,0},{5,1},{6,2},{7,3},{8,4},{9,5},{1... | collective-permute-start | bytes 1400840 | tf_op jit(solution)/shard_map/ppermute | solution.py:53
  72.4 104.0 %collective-permute-start.1 = (bf16[4,456,128]{2,1,0:T(8,128)(2,1)}, bf16[4,456,128]{2,1,0:T(8,128)(2,1)S(1)}, u32[]{:S(2)}, u32[]{:S(2)}) collective-permute-start(bf16[4,456,128]{2,1,0:T(8,128)(2,1)} %get-tuple-element.81), channel_id=1, source_target_pairs={{0,8},{1,9},{2,10},{3,11},{4,12},{5,13},{6,14},{7,15},{8,0},{9,1},... | collective-permute-start | bytes 1400840 | tf_op jit(solution)/shard_map/ppermute | solution.py:53
  79.6 96.8 %collective-permute-start = (bf16[4,456,128]{2,1,0:T(8,128)(2,1)}, bf16[4,456,128]{2,1,0:T(8,128)(2,1)S(1)}, u32[]{:S(2)}, u32[]{:S(2)}) collective-permute-start(bf16[4,456,128]{2,1,0:T(8,128)(2,1)} %get-tuple-element.82), channel_id=1, source_target_pairs={{0,4},{1,5},{2,6},{3,7},{4,8},{5,9},{6,10},{7,11},{8,12},{9,13},{1... | collective-permute-start | bytes 1400840 | tf_op jit(solution)/shard_map/ppermute | solution.py:53
  127.3 3.7 %copy-start.5 = (bf16[16,736,128]{2,1,0:T(8,128)(2,1)S(1)}, bf16[16,736,128]{2,1,0:T(8,128)(2,1)}, u32[]{:S(2)}) copy-start(bf16[16,736,128]{2,1,0:T(8,128)(2,1)} %all-gather.5.cloned.1.call-done) | copy-start | bytes 9043972
  130.9 77.6 %copy-start = (s32[896,1]{1,0:T(8,128)S(1)}, s32[896,1]{1,0:T(8,128)}, u32[]{:S(2)}) copy-start(s32[896,1]{1,0:T(8,128)} %get-tuple-element.69.refs_2_) | copy-start | bytes 10756
  210.0 10.9 %all-to-all-start.4 = ((bf16[4,224,128]{2,1,0:T(8,128)(2,1)}), bf16[4,224,128]{2,1,0:T(8,128)(2,1)S(1)}, u32[]{:S(2)}, u32[]{:S(2)}) async-start(bf16[4,224,128]{2,1,0:T(8,128)(2,1)} %spread.1), calls=%async_computation.4 | async-start | bytes 458752 | tf_op jit(solution)/shard_map/all_to_all | solution.py:396
  214.6 2.7 %copy-start.1 = (s32[224,1]{1,0:T(8,128)S(1)}, s32[224,1]{1,0:T(8,128)}, u32[]{:S(2)}) copy-start(s32[224,1]{1,0:T(8,128)} %get-tuple-element.76.refs_5_) | copy-start | bytes 2692
Sparse Core Ops, SparseCore 0:
  67.5 59.7 all-gather.4

commit v4 on v3

--- a/solution.py
+++ b/solution.py
@@ -311,7 +311,8 @@
     out_ref[...] = jnp.sum(parts_ref[...].astype(jnp.float32), axis=0).astype(jnp.bfloat16)
 
 
-def gradient_kernel(rows_ref, returned_ref, out_ref):
+def update_kernel(rows_ref, returned_ref, *refs):
+    recv_ref, w_ref, m_ref, v_ref = refs[RING:]
     blocks, lines, lanes = returned_ref.shape
     part = lines // 9
     total = 0.0
@@ -323,15 +324,11 @@
             for c in range(2)
         ]
         total += dot(jnp.concatenate(scaled, axis=1), rows_ref[side], CONTRACT_FIRST)
-    out_ref[...] = total[: out_ref.shape[0]]
-
-
-def update_kernel(gradient_ref, *refs):
-    recv_ref, w_ref, m_ref, v_ref = refs[RING:]
+    total = total[: w_ref.shape[0]]
     arrived = Arrived(refs[:RING], recv_ref[...], 3)
     for c in range(CHUNKS):
         piece = slice(c * LANES, (c + 1) * LANES)
-        gradient = gradient_ref[:, piece]
+        gradient = total[:, piece]
         weight = arrived.piece(0, c)
         one_next = beta_one * arrived.piece(1, c) + (1.0 - beta_one) * gradient
         two_next = beta_two * arrived.piece(2, c) + (1.0 - beta_two) * gradient * gradient
@@ -482,14 +479,12 @@
         scalars=1,
     )
     combined = call(sum_kernel, "sum", shape(width, tok_rows), exchange(spread, "dp", NEAR)).T
-    gradient = call(
-        gradient_kernel, "gradient", shape(width, hidden, dtype=jnp.float32), rows_now, returned
-    )
     new_weight, new_one, new_two = call(
         update_kernel,
         "update",
         (shape(width, hidden),) * 3,
-        gradient,
+        rows_now,
+        returned,
         *state_got,
         recv,
     )

time: 229 us -> 229 us (level)
    pallas_call x9 -> x8, Pallas kernels: 24.3 us -> 24.1 us  [call(): pl.pallas_call(body, out_shape=out_shape, in_specs=specs + [pl.BlockSpec(...]
where the time goes in v4:
time: 229 us; the launch traced here: 228 us
  blocking collectives  110 us (48%)
  waiting for transfers between devices  44.5 us (19%)
  starting transfers between devices  30.2 us (13%)
  Pallas kernels  24.1 us (11%)
  between operations  14.8 us (6%)
  local copies, waits for them, and re-layouts  3.88 us (2%)
    all_gather x2, blocking collectives, gather_far(): return lax.all_gather(piece, 'dp', axis=0, axis_index_groups=FAR)  69.9 us
    all_gather x1, waiting for transfers between devices, gather_near(): return lax.all_gather(piece, 'dp', axis=0, axis_index_groups=NEAR)  44.4 us
    all_to_all x1, blocking collectives, exchange(): lax.all_to_all(array, axis, split_axis=0, concat_axis=0, tiled=True, axis...  40.5 us
    pallas_call x8, Pallas kernels, call(): pl.pallas_call(body, out_shape=out_shape, in_specs=specs + [pl.BlockSpec(...  24.1 us
    all_to_all x3, starting transfers between devices, exchange(): lax.all_to_all(array, axis, split_axis=0, concat_axis=0, tiled=True, axis...  17.7 us
    ppermute x3, starting transfers between devices, send_far(): return lax.ppermute(piece, 'dp', pairs)  12.5 us
  transfers between devices with their start and end apart: 7, of which 1 were waited for; matrix products, arithmetic and copies ran while one was open for 1% of the time, Pallas kernels for 9%

profile of v4, /device:TPU:90, one launch (start us, length us, event | category | flops | bytes accessed | tf_op | source)
XLA Modules:
  0.0 228.3 jit_solution(18229077364135563514)
XLA Ops:
  7.2 0.0 copy-start.3
  7.2 0.8 copy-done.3
  8.0 0.0 copy-start.4
  8.0 0.7 copy-done.4
  8.7 1.3 dispatch.1
  10.0 8.1 %all-to-all-start.2 = ((bf16[32,16,128]{2,1,0:T(8,128)(2,1)}), bf16[32,16,128]{2,1,0:T(8,128)(2,1)S(1)}, u32[]{:S(2)}, u32[]{:S(2)}) async-start(bf16[32,16,128]{2,1,0:T(8,128)(2,1)} %get-tuple-element.60), calls=%async_computation.2 | async-start | bytes 262144 | tf_op jit(solution)/shard_map/all_to_all | solution.py:393
  18.1 6.6 %pack.1 = (bf16[16,456,128]{2,1,0:T(8,128)(2,1)}, s32[224,1]{1,0:T(8,128)}, s32[224,1]{1,0:T(8,128)}, s32[896,1]{1,0:T(8,128)}) custom-call(s32[1]{0:T(128)} %bitcast.refs_0_, s32[28,128]{1,0:T(8,128)} %bitcast.49, s32[28,128]{1,0:T(8,128)} %bitcast.50, bf16[304,1024]{1,0:T(8,128)(2,1)} %bitcast.36, bf16[304,1024]{1,0:T(8,128)(2,1)} %bitcast.41, ...), custom_call_target="tpu_custom_call" | custom-call | bytes 1024 | tf_op jit(solution)/shard_map/pack/pallas_call | solution.py:354
  24.7 0.0 all-to-all-done.2
  24.7 0.0 copy-start.7
  24.7 5.0 %all-to-all-start.3 = ((bf16[4,4,456,128]{3,2,1,0:T(8,128)(2,1)}), bf16[4,4,456,128]{3,2,1,0:T(8,128)(2,1)S(1)}, u32[]{:S(2)}, u32[]{:S(2)}) async-start(bf16[4,4,456,128]{3,2,1,0:T(8,128)(2,1)} %bitcast.40), calls=%async_computation.3 | async-start | bytes 3735552 | tf_op jit(solution)/shard_map/all_to_all | solution.py:393
  29.7 0.0 all-gather.5.cloned.1.call-start
  29.7 0.0 copy-done.7
  29.7 37.6 %all-gather = bf16[2944,128]{1,0:T(8,128)(2,1)} all-gather(bf16[736,128]{1,0:T(8,128)(2,1)S(1)} %pad_maximum_fusion), channel_id=2, replica_groups={{0,4,8,12},{1,5,9,13},{2,6,10,14},{3,7,11,15},{16,20,24,28},{17,21,25,2..., dimensions={0}, use_global_device_ids=true | all-gather | bytes 942080 | tf_op jit(solution)/shard_map/all_gather | solution.py:40
  67.3 0.0 all-to-all-done.3
  67.3 0.0 all-gather.5.cloned.1.call-update
  67.3 0.0 copy-start.2
  67.3 0.0 copy-start.8
  67.4 1.1 slice_bitcast_fusion
  68.5 0.0 copy-start.6
  68.5 3.9 %collective-permute-start.2 = (bf16[4,456,128]{2,1,0:T(8,128)(2,1)}, bf16[4,456,128]{2,1,0:T(8,128)(2,1)S(1)}, u32[]{:S(2)}, u32[]{:S(2)}) collective-permute-start(bf16[4,456,128]{2,1,0:T(8,128)(2,1)} %get-tuple-element.80), channel_id=1, source_target_pairs={{0,12},{1,13},{2,14},{3,15},{4,0},{5,1},{6,2},{7,3},{8,4},{9,5},{1... | collective-permute-start | bytes 1400840 | tf_op jit(solution)/shard_map/ppermute | solution.py:53
  72.4 7.2 %collective-permute-start.1 = (bf16[4,456,128]{2,1,0:T(8,128)(2,1)}, bf16[4,456,128]{2,1,0:T(8,128)(2,1)S(1)}, u32[]{:S(2)}, u32[]{:S(2)}) collective-permute-start(bf16[4,456,128]{2,1,0:T(8,128)(2,1)} %get-tuple-element.81), channel_id=1, source_target_pairs={{0,8},{1,9},{2,10},{3,11},{4,12},{5,13},{6,14},{7,15},{8,0},{9,1},... | collective-permute-start | bytes 1400840 | tf_op jit(solution)/shard_map/ppermute | solution.py:53
  79.6 1.4 collective-permute-start
  81.0 1.2 slice.15
  82.8 44.4 %all-gather.5.cloned.1.call-done = bf16[16,736,128]{2,1,0:T(8,128)(2,1)} async-done(((bf16[4,736,128]{2,1,0:T(8,128)(2,1)}), bf16[16,736,128]{2,1,0:T(8,128)(2,1)}) %all-gather.5.cloned.1.call-update) | async-done | bytes 3014672 | tf_op jit(solution)/shard_map/all_gather | solution.py:44
  127.3 0.0 copy-start.5
  127.3 0.0 copy-done.2
  127.3 0.0 copy-done.8
  127.3 3.6 %scale.1 = bf16[32,64,128]{2,1,0:T(8,128)(2,1)S(1)} custom-call(bf16[4,4,736,128]{3,2,1,0:T(8,128)(2,1)} %bitcast.33, s32[224,1]{1,0:T(8,128)S(1)} %copy-done.2, f32[4,128]{1,0:T(4,128)S(1)} %bitcast.46, s32[4,128]{1,0:T(4,128)S(1)} %get-tuple-element.65.refs_3_), custom_call_target="tpu_custom_call" | custom-call | bytes 1024 | tf_op jit(solution)/shard_map/scale/pallas_call | solution.py:354
  130.9 0.0 copy-done.6
  130.9 0.0 copy-done.5
  130.9 0.0 copy-start
  131.0 45.4 %conditional.1 = (bf16[2,512,1024]{2,1,0:T(8,128)(2,1)}, bf16[304,128]{1,0:T(8,128)(2,1)S(1)}, bf16[32,144,128]{2,1,0:T(8,128)(2,1)}) conditional(s32[]{:T(128)} %bitcast.1, (bf16[4,4,736,128]{3,2,1,0:T(8,128)(2,1)S(1)}, bf16[304,1024]{1,0:T(8,128)(2,1)S(1)}, bf16[32,64,128]{2,1,0:T(8,128)(2,1)S(1)}, f32[4,128]{1,0:T(4,128)S(1)}, ...), branch_computations={%region_0.0_spmd, %region_1.0_spmd} | conditional | bytes 2361368 | solution.py:461
  131.2 2.6 %forward.1 = (bf16[2,512,1024]{2,1,0:T(8,128)(2,1)}, bf16[32,144,128]{2,1,0:T(8,128)(2,1)S(1)}) custom-call(bf16[4,4,736,128]{3,2,1,0:T(8,128)(2,1)S(1)} %get-tuple-element.27.refs_0_, bf16[304,1024]{1,0:T(8,128)(2,1)S(1)} %get-tuple-element.28.refs_1_, bf16[32,64,128]{2,1,0:T(8,128)(2,1)S(1)} %get-tuple-element.29.refs_2_), custom_call_target="tpu_custom_call" | custom-call | bytes 1024 | tf_op jit(solution)/shard_map/cond/branch_1_fun/forward/pallas_call | solution.py:354
  133.8 40.5 %all_to_all.24.refs_0_ = bf16[32,144,128]{2,1,0:T(8,128)(2,1)} all-to-all(bf16[32,144,128]{2,1,0:T(8,128)(2,1)S(1)} %get-tuple-element.31), channel_id=1, replica_groups=mesh['expert'=32,'dp'=16] {'expert'}, dimensions={0} | all-to-all | bytes 2359296 | tf_op jit(solution)/shard_map/cond/branch_1_fun/all_to_all | solution.py:393
  174.2 1.9 combine.3
  176.4 0.0 copy-start.1
  176.4 0.0 collective-permute-done.2.refs_5_
  176.4 0.0 collective-permute-done.1.refs_4_
  176.4 0.0 collective-permute-done.refs_3_
  176.4 32.3 %all-gather.2 = bf16[1216,128]{1,0:T(8,128)(2,1)S(1)} all-gather(bf16[304,128]{1,0:T(8,128)(2,1)S(1)} %get-tuple-element.68), channel_id=4, replica_groups={{0,4,8,12},{1,5,9,13},{2,6,10,14},{3,7,11,15},{16,20,24,28},{17,21,25,2..., dimensions={0}, use_global_device_ids=true | all-gather | bytes 389120 | tf_op jit(solution)/shard_map/all_gather | solution.py:40
  208.7 0.0 copy-done
  208.7 1.4 spread.1
  210.1 4.6 %all-to-all-start.4 = ((bf16[4,224,128]{2,1,0:T(8,128)(2,1)}), bf16[4,224,128]{2,1,0:T(8,128)(2,1)S(1)}, u32[]{:S(2)}, u32[]{:S(2)}) async-start(bf16[4,224,128]{2,1,0:T(8,128)(2,1)} %spread.1), calls=%async_computation.4 | async-start | bytes 458752 | tf_op jit(solution)/shard_map/all_to_all | solution.py:393
  214.7 0.0 copy-done.1
  214.7 6.0 %update.1 = (bf16[224,1024]{1,0:T(8,128)(2,1)}, bf16[224,1024]{1,0:T(8,128)(2,1)}, bf16[224,1024]{1,0:T(8,128)(2,1)}) custom-call(bf16[2,512,1024]{2,1,0:T(8,128)(2,1)} %get-tuple-element.70.refs_0_, bf16[32,144,128]{2,1,0:T(8,128)(2,1)} %get-tuple-element.71.refs_1_, bf16[4,456,128]{2,1,0:T(8,128)(2,1)S(1)} %get-tuple-element.72.refs_2_, ...), custom_call_target="tpu_custom_call" | custom-call | bytes 1024 | tf_op jit(solution)/shard_map/update/pallas_call | solution.py:354
  220.8 0.0 all-to-all-done.4.refs_0_
  220.8 0.7 sum.1
  (1 shorter events, 0.0 us)
Async XLA Ops:
  7.2 0.8 copy-start.3
  8.0 0.7 copy-start.4
  10.0 14.7 %all-to-all-start.2 = ((bf16[32,16,128]{2,1,0:T(8,128)(2,1)}), bf16[32,16,128]{2,1,0:T(8,128)(2,1)S(1)}, u32[]{:S(2)}, u32[]{:S(2)}) async-start(bf16[32,16,128]{2,1,0:T(8,128)(2,1)} %get-tuple-element.60), calls=%async_computation.2 | async-start | bytes 262144 | tf_op jit(solution)/shard_map/all_to_all | solution.py:393
  24.7 5.0 %copy-start.7 = (bf16[128,224]{0,1:T(8,128)(2,1)S(1)}, bf16[128,224]{0,1:T(8,128)(2,1)}, u32[]{:S(2)}) copy-start(bf16[128,224]{0,1:T(8,128)(2,1)} %param.14) | copy-start | bytes 172036
  24.7 42.6 %all-to-all-start.3 = ((bf16[4,4,456,128]{3,2,1,0:T(8,128)(2,1)}), bf16[4,4,456,128]{3,2,1,0:T(8,128)(2,1)S(1)}, u32[]{:S(2)}, u32[]{:S(2)}) async-start(bf16[4,4,456,128]{3,2,1,0:T(8,128)(2,1)} %bitcast.40), calls=%async_computation.3 | async-start | bytes 3735552 | tf_op jit(solution)/shard_map/all_to_all | solution.py:393
  29.7 97.6 %all-gather.5.cloned.1.call-start = ((), (), s32[]{:S(2)}) async-start(), calls=%async_computation.5 | async-start | bytes 3768320 | tf_op jit(solution)/shard_map/all_gather | solution.py:44
  67.3 59.9 %copy-start.2 = (s32[224,1]{1,0:T(8,128)S(1)}, s32[224,1]{1,0:T(8,128)}, u32[]{:S(2)}) copy-start(s32[224,1]{1,0:T(8,128)} %get-tuple-element.64.refs_1_) | copy-start | bytes 2692
  67.3 59.9 %copy-start.8 = (f32[128,4]{0,1:T(4,128)S(1)}, f32[128,4]{0,1:T(4,128)}, u32[]{:S(2)}) copy-start(f32[128,4]{0,1:T(4,128)} %param.13) | copy-start | bytes 6148
  68.5 62.4 %copy-start.6 = (bf16[1,304,1024]{2,1,0:T(8,128)(2,1)S(1)}, bf16[1,304,1024]{2,1,0:T(8,128)(2,1)}, u32[]{:S(2)}) copy-start(bf16[1,304,1024]{2,1,0:T(8,128)(2,1)} %param.15) | copy-start | bytes 1867780
  68.5 107.9 %collective-permute-start.2 = (bf16[4,456,128]{2,1,0:T(8,128)(2,1)}, bf16[4,456,128]{2,1,0:T(8,128)(2,1)S(1)}, u32[]{:S(2)}, u32[]{:S(2)}) collective-permute-start(bf16[4,456,128]{2,1,0:T(8,128)(2,1)} %get-tuple-element.80), channel_id=1, source_target_pairs={{0,12},{1,13},{2,14},{3,15},{4,0},{5,1},{6,2},{7,3},{8,4},{9,5},{1... | collective-permute-start | bytes 1400840 | tf_op jit(solution)/shard_map/ppermute | solution.py:53
  72.4 104.0 %collective-permute-start.1 = (bf16[4,456,128]{2,1,0:T(8,128)(2,1)}, bf16[4,456,128]{2,1,0:T(8,128)(2,1)S(1)}, u32[]{:S(2)}, u32[]{:S(2)}) collective-permute-start(bf16[4,456,128]{2,1,0:T(8,128)(2,1)} %get-tuple-element.81), channel_id=1, source_target_pairs={{0,8},{1,9},{2,10},{3,11},{4,12},{5,13},{6,14},{7,15},{8,0},{9,1},... | collective-permute-start | bytes 1400840 | tf_op jit(solution)/shard_map/ppermute | solution.py:53
  79.6 96.8 %collective-permute-start = (bf16[4,456,128]{2,1,0:T(8,128)(2,1)}, bf16[4,456,128]{2,1,0:T(8,128)(2,1)S(1)}, u32[]{:S(2)}, u32[]{:S(2)}) collective-permute-start(bf16[4,456,128]{2,1,0:T(8,128)(2,1)} %get-tuple-element.82), channel_id=1, source_target_pairs={{0,4},{1,5},{2,6},{3,7},{4,8},{5,9},{6,10},{7,11},{8,12},{9,13},{1... | collective-permute-start | bytes 1400840 | tf_op jit(solution)/shard_map/ppermute | solution.py:53
  127.3 3.7 %copy-start.5 = (bf16[16,736,128]{2,1,0:T(8,128)(2,1)S(1)}, bf16[16,736,128]{2,1,0:T(8,128)(2,1)}, u32[]{:S(2)}) copy-start(bf16[16,736,128]{2,1,0:T(8,128)(2,1)} %all-gather.5.cloned.1.call-done) | copy-start | bytes 9043972
  130.9 77.8 %copy-start = (s32[896,1]{1,0:T(8,128)S(1)}, s32[896,1]{1,0:T(8,128)}, u32[]{:S(2)}) copy-start(s32[896,1]{1,0:T(8,128)} %get-tuple-element.69.refs_2_) | copy-start | bytes 10756
  176.4 38.4 %copy-start.1 = (s32[224,1]{1,0:T(8,128)S(1)}, s32[224,1]{1,0:T(8,128)}, u32[]{:S(2)}) copy-start(s32[224,1]{1,0:T(8,128)} %get-tuple-element.76.refs_6_) | copy-start | bytes 2692
  210.1 10.7 %all-to-all-start.4 = ((bf16[4,224,128]{2,1,0:T(8,128)(2,1)}), bf16[4,224,128]{2,1,0:T(8,128)(2,1)S(1)}, u32[]{:S(2)}, u32[]{:S(2)}) async-start(bf16[4,224,128]{2,1,0:T(8,128)(2,1)} %spread.1), calls=%async_computation.4 | async-start | bytes 458752 | tf_op jit(solution)/shard_map/all_to_all | solution.py:393
Sparse Core Ops, SparseCore 0:
  67.5 59.7 all-gather.4
